TPU v7x, 32 devices: a whole 2x2x4 slice. The times are simulated.
32 devices in a mesh: ctx: 8 (over y, x, core), fsdp: 4 (over z).
Axes of the slice: x: 2, y: 2, z: 4, core: 2. Of those that a mesh axis runs over, the one named last changes fastest.
Arguments:
- tokens: bfloat16 [4, 3072, 960], P('fsdp', 'ctx'), may hold values from -6 to 6
- attn_gain: bfloat16 [960], P('fsdp'), may hold values from 0.25 to 1.75
- query_weight: bfloat16 [960, 960], P('fsdp'), may hold values from -0.1875 to 0.1875
- key_weight: bfloat16 [960, 320], P('fsdp'), may hold values from -0.1875 to 0.1875
- value_weight: bfloat16 [960, 320], P('fsdp'), may hold values from -0.1875 to 0.1875
- out_weight: bfloat16 [960, 960], P('fsdp'), may hold values from -3.5 to 3.5
- mlp_gain: bfloat16 [960], P('fsdp'), may hold values from 0.25 to 1.75
- gate_weight: bfloat16 [960, 2560], P('fsdp'), may hold values from -0.1875 to 0.1875
- up_weight: bfloat16 [960, 2560], P('fsdp'), may hold values from -0.1875 to 0.1875
- down_weight: bfloat16 [2560, 960], P('fsdp'), may hold values from -0.125 to 0.125
- cotangent: bfloat16 [4, 3072, 960], P('fsdp', 'ctx'), may hold values from -6 to 6
- cont_lengths: int32 [4, 2], P('fsdp'), may hold values from 1 to 1024, 1536 in all within a row
- block_deal: int32 [16], replicated, may hold values from 0 to 15, as said below
Outputs:
- output: bfloat16 [4, 3072, 960], P('fsdp', 'ctx')
- tokens_grad: bfloat16 [4, 3072, 960], P('fsdp', 'ctx')
- attn_gain_grad: float32 [960], P('fsdp')
- query_grad: float32 [960, 960], P('fsdp')
- key_grad: float32 [960, 320], P('fsdp')
- value_grad: float32 [960, 320], P('fsdp')
- out_grad: float32 [960, 960], P('fsdp')
- mlp_gain_grad: float32 [960], P('fsdp')
- gate_grad: float32 [960, 2560], P('fsdp')
- up_grad: float32 [960, 2560], P('fsdp')
- down_grad: float32 [2560, 960], P('fsdp')
Inputs may be any that keep to these rules, and one draw needn't show every extreme that they name: `block_deal`: stored blocks 2 c and 2 c + 1 hold natural blocks k and 15 - k, in either order, for some k; every block appears once. `cont_lengths`: each group's 2 lengths add up to 1536.
All inputs are finite; a program needn't handle non-finite values.
Results may differ from a plain program's by a relative error of at most 0.02.
Values may be sent and summed in bfloat16 or wider, within the bound.
A program may use at most 192 MiB of HBM per device.

v0:
```python
import functools

import jax
import jax.numpy as jnp
from jax import lax
from jax.experimental import pallas as pl
from jax.experimental.pallas import tpu as pltpu
from jax.sharding import PartitionSpec as P

HD = 64
LANES = 128
EPSILON = 1e-05
THETA = 100000.0
MASKED = -1e30
LOG2E = 1.4426950408889634
VMEM_LIMIT = 63 * 1024 * 1024
F32 = jnp.float32
BF16 = jnp.bfloat16


def nt(left, right):
    return lax.dot_general(left, right, (((1,), (1,)), ((), ())), preferred_element_type=F32)


def nn(left, right):
    return lax.dot_general(left, right, (((1,), (0,)), ((), ())), preferred_element_type=F32)


def tn(left, right):
    return lax.dot_general(left, right, (((0,), (0,)), ((), ())), preferred_element_type=F32)


def rope_tile(tile, cos, sin):
    lane = lax.broadcasted_iota(jnp.int32, tile.shape, 1) % HD
    partner = jnp.where(
        lane < HD // 2,
        pltpu.roll(tile, LANES - HD // 2, 1),
        pltpu.roll(tile, HD // 2, 1),
    )
    return tile * cos + partner * sin


def head_of(tiles, index):
    start = (index % 2) * HD
    return tiles[index // 2][:, start : start + HD]


MESH = pl.DeviceIdType.MESH
ATTN, FF, DOWN = 0, 1, 2
CORE, FIRST, SECOND = -1, -2, -3


class Links:
    def __init__(self, core, fsdp, send, recv, plan):
        self.core = core
        self.fsdp = fsdp
        self.ctx = lax.axis_index("ctx")
        self.z = lax.axis_index("fsdp")
        self.chip = self.ctx // 2
        self.first = 1 if core == 0 else 2
        self.second = 3 - self.first
        self.send_sem, self.recv_sem = send, recv
        self.plan = plan
        self.open = []

    def target(self, hop):
        if hop == CORE:
            return (lax.bitwise_xor(self.ctx, 1), self.z)
        if hop == FIRST:
            return (lax.bitwise_xor(self.ctx, 2 * self.first), self.z)
        if hop == SECOND:
            return (lax.bitwise_xor(self.ctx, 2 * self.second), self.z)
        return (self.ctx, lax.bitwise_xor(self.z, hop))

    def copy(self, key, hop, src, dst):
        slot = self.plan.setdefault(key, len(self.plan))
        return pltpu.make_async_remote_copy(
            src_ref=src,
            dst_ref=dst,
            send_sem=self.send_sem.at[slot],
            recv_sem=self.recv_sem.at[slot],
            device_id=self.target(hop),
            device_id_type=MESH,
        )

    def send(self, key, hop, src, dst):
        copy = self.copy(key, hop, src, dst)
        copy.start()
        self.open.append((key, getattr(src, "ref", src), src.shape))

    def landed(self, key, dst):
        self.copy(key, CORE, dst, dst).wait_recv()

    def drain(self):
        for key, base, shape in self.open:
            at = (0,) * (len(base.shape) - len(shape)) + tuple(pl.ds(0, size) for size in shape)
            self.copy(key, CORE, base.at[at], base.at[at]).wait_send()


def greet(hops, fsdp):
    ctx, z = lax.axis_index("ctx"), lax.axis_index("fsdp")
    barrier = pltpu.get_barrier_semaphore()
    targets = [(lax.bitwise_xor(ctx, h), z) for h in (1, 2, 4)]
    if "z" in hops:
        targets += [(ctx, lax.bitwise_xor(z, d)) for d in range(1, fsdp)]
    for target in targets:
        pl.semaphore_signal(barrier, inc=1, device_id=target, device_id_type=MESH)
    pl.semaphore_wait(barrier, len(targets))


def by_core(program):
    for core in (0, 1):
        pl.when(lax.axis_index("ctx") % 2 == core)(functools.partial(program, core))


def sub(base, size, unit):
    return pl.ds(pl.multiple_of(base, unit), size)


def lanes(ref, tiles, rows=slice(None)):
    return jnp.concatenate([ref[t, rows, :] for t in tiles], axis=1)


def pack_tiles(parts):
    matrix = jnp.concatenate(parts, axis=1)
    short = -matrix.shape[1] % LANES
    if short:
        matrix = jnp.concatenate([matrix, jnp.zeros((matrix.shape[0], short), matrix.dtype)], axis=1)
    return [matrix[:, t * LANES : (t + 1) * LANES] for t in range(matrix.shape[1] // LANES)]


class Share:
    def __init__(self, name, core, shard):
        self.name, self.core = name, core
        self.shard = shard
        self.offset, self.rows = 0, shard
        if name == ATTN:
            half = -(-shard // 32) * 16
            self.offset, self.rows = (0, half) if core == 0 else (half, shard - half)

    def at(self, ref, zi, q):
        rows = sub(zi * self.shard + self.offset, self.rows, 16)
        if self.name == ATTN:
            return ref.at[pl.ds(q * (ref.shape[0] // 4), ref.shape[0] // 4), rows]
        if self.name == FF:
            return ref.at[self.core, pl.ds(q * (ref.shape[1] // 4), ref.shape[1] // 4), rows]
        return ref.at[2 * q + self.core, rows]

    def buffer(self, ref):
        return ref.at[:, pl.ds(0, self.rows)] if self.name == ATTN else ref


PACKAGES = (ATTN, FF, DOWN)
FINISH = 0


def both_cores(make):
    tables = [make(0), make(1)]

    def run(*names):
        for core in (0, 1):
            def program(core=core):
                for name in names:
                    tables[core][name]()

            pl.when(lax.axis_index("ctx") % 2 == core)(program)

    return run


def weight_stages(core, fsdp, plan, refs, send, recv):
    links = Links(core, fsdp, send, recv, plan)
    z, chip = links.z, links.chip
    near, far = lax.bitwise_xor(chip, links.first), lax.bitwise_xor(chip, links.second)
    corner = lax.bitwise_xor(chip, 3)
    shards = {ATTN: refs[ATTN].shape[1] // fsdp, FF: refs[FF].shape[2] // fsdp, DOWN: refs[DOWN].shape[1] // fsdp}
    mine = {k: Share(k, core, shards[k]) for k in PACKAGES}
    twin = {k: Share(k, 1 - core, shards[k]) for k in PACKAGES}
    stages = {}

    def over_z(k):
        here = mine[k].at(refs[k], z, chip)
        for d in range(1, fsdp):
            links.send((k, "z", d), d, here, here)

    def spread(k):
        for d in range(1, fsdp):
            piece = mine[k].at(refs[k], lax.bitwise_xor(z, d), chip)
            links.landed((k, "z", d), piece)
            links.send((k, FIRST, d), FIRST, piece, piece)
            links.send((k, SECOND, d), SECOND, piece, piece)
            links.send((k, CORE, d, 0), CORE, piece, piece)

    def forward(k):
        for d in range(1, fsdp):
            piece = mine[k].at(refs[k], lax.bitwise_xor(z, d), near)
            links.landed((k, FIRST, d), piece)
            links.send((k, "corner", d), SECOND, piece, piece)
            links.send((k, CORE, d, 1), CORE, piece, piece)

    def pass_some(k, i, what, q):
        for d in range(1, fsdp):
            piece = mine[k].at(refs[k], lax.bitwise_xor(z, d), q)
            links.landed((k, what, d), piece)
            links.send((k, CORE, d, i), CORE, piece, piece)

    def pass_far(k):
        pass_some(k, 2, SECOND, far)

    def pass_corner(k):
        pass_some(k, 3, "corner", corner)

    def finish_some(k, i, q):
        for d in range(1, fsdp):
            links.landed((k, CORE, d, i), twin[k].at(refs[k], lax.bitwise_xor(z, d), q))

    def finish(k):
        for i in range(4):
            stages[FINISH, k, i]()

    for k in PACKAGES:
        for i, q in ((0, chip), (1, far), (2, near), (3, corner)):
            stages[FINISH, k, i] = functools.partial(finish_some, k, i, q)
    for k in PACKAGES:
        for fn in (over_z, spread, forward, pass_far, pass_corner, finish):
            stages[fn.__name__, k] = functools.partial(fn, k)

    def gains_out():
        for d in range(1, fsdp):
            links.send(("gains", d), d, refs["gains"].at[z], refs["gains"].at[z])

    def gains_in():
        for d in range(1, fsdp):
            links.landed(("gains", d), refs["gains"].at[lax.bitwise_xor(z, d)])

    stages["gains_out"], stages["gains_in"], stages["drain"] = gains_out, gains_in, links.drain
    return stages


def kv_stages(core, plan, kv_all, send, recv):
    links = Links(core, 1, send, recv, plan)
    ctx = links.ctx
    near = lax.bitwise_xor(ctx, 2 * links.first)
    far = lax.bitwise_xor(ctx, 2 * links.second)
    corner = lax.bitwise_xor(ctx, 6)

    def start():
        for b in range(2):
            piece = kv_all.at[ctx, b]
            links.send(("kv first", b), FIRST, piece, piece)
            links.send(("kv second", b), SECOND, piece, piece)
            links.send(("kv core", 0, b), CORE, piece, piece)

    def forward():
        for b in range(2):
            piece = kv_all.at[near, b]
            links.landed(("kv first", b), piece)
            links.send(("kv corner", b), SECOND, piece, piece)
            links.send(("kv core", 1, b), CORE, piece, piece)

    def pass_on():
        for i, (what, owner) in enumerate((("kv second", far), ("kv corner", corner))):
            for b in range(2):
                piece = kv_all.at[owner, b]
                links.landed((what, b), piece)
                links.send(("kv core", 2 + i, b), CORE, piece, piece)

    def finish():
        for i, owner in ((0, ctx), (1, far), (2, near), (3, corner)):
            for b in range(2):
                links.landed(("kv core", i, b), kv_all.at[lax.bitwise_xor(owner, 1), b])

    return {"start": start, "forward": forward, "pass_on": pass_on, "finish": finish, "drain": links.drain}


def store_projection(sizes, raw_tiles, cos, sin, q_ref, kv_at):
    heads, kvh, block = sizes
    share = heads // kvh
    tiles = [rope_tile(raw_tiles[j], cos, sin).astype(BF16) for j in range((heads + kvh) // 2)]
    tiles += [raw_tiles[j].astype(BF16) for j in range((heads + kvh) // 2, len(raw_tiles))]

    def head(index):
        start = (index % 2) * HD
        return tiles[index // 2][:, start : start + HD]

    zero = jnp.zeros((block, HD), BF16)
    for h in range(heads):
        piece = head(h) * jnp.asarray(0.125, BF16)
        g, i = h // share, h % share
        for b in range(2):
            q_ref[g, b, i * block : (i + 1) * block, :] = jnp.concatenate(
                [piece[b * block : (b + 1) * block], zero], axis=1
            )
    for g in range(kvh):
        pair = jnp.concatenate([head(heads + g), head(heads + kvh + g)], axis=1)
        for b in range(2):
            kv_at(b, g)[...] = pair[b * block : (b + 1) * block]


def rms_inverse(x):
    return lax.rsqrt(jnp.mean(x * x, axis=1, keepdims=True) + EPSILON)


def natural_blocks(deal_ref, c):
    one, two = deal_ref[2 * c], deal_ref[2 * c + 1]
    return jnp.minimum(one, two), jnp.maximum(one, two)


def segment_start(lengths_ref, offset):
    start = jnp.zeros_like(offset)
    ending = 0
    for c in range(lengths_ref.shape[1]):
        ending = ending + lengths_ref[0, c]
        start = jnp.where(offset >= ending, ending, start)
    return start


def ordered(flip, rows):
    half = rows.shape[0] // 2
    return jnp.where(flip, jnp.concatenate([rows[half:], rows[:half]], axis=0), rows)


def first_keys(n, deal_ref, lengths_ref, block, rows):
    _, last = natural_blocks(deal_ref, lax.axis_index("ctx"))
    offset = (last - n) * block + lax.rem(lax.broadcasted_iota(jnp.int32, (8, rows), 1), block)
    return segment_start(lengths_ref, offset)


def attend_masks(n, deal_ref, start_ref, block, rows):
    key = lax.broadcasted_iota(jnp.int32, (block, rows), 0)

    def own(b):
        allowed = key <= lax.rem(lax.broadcasted_iota(jnp.int32, (block, rows), 1), block)
        if b == 0:
            return allowed
        _, last = natural_blocks(deal_ref, lax.axis_index("ctx"))
        return allowed & (key >= start_ref[0:1, :] - (last - n) * block)

    def other(at):
        mine, _ = natural_blocks(deal_ref, lax.axis_index("ctx"))
        first, last = natural_blocks(deal_ref, at)
        kind = jnp.where(first >= mine, 1, 0)
        bound = jnp.where(kind == 0, -1, start_ref[0:1, :] - (last - n) * block)
        return kind, key >= bound

    return own, other


def attend_step(n, me, g, j, deal_ref, start_ref, q_ref, kv_ref, top_ref, acc_ref):
    block = kv_ref.shape[3]
    rows = q_ref.shape[2]
    value_lane = lax.broadcasted_iota(jnp.int32, (block, LANES), 1) >= HD
    own_mask, other_mask = attend_masks(n, deal_ref, start_ref, block, rows)

    def scores(kind, tile, mask):
        s = nt(tile, q_ref[g, kind])
        return s if mask is None else jnp.where(mask, s, MASKED)

    def weigh(s, top, tile):
        p = jnp.exp2((s - top) * LOG2E).astype(BF16)
        return tn(jnp.where(value_lane, tile, jnp.asarray(1, BF16)), p)

    def own():
        own0, own1 = kv_ref[me, 0, g], kv_ref[me, 1, g]
        s0 = scores(0, own0, own_mask(0))
        top0 = jnp.max(s0, axis=0, keepdims=True)
        acc_ref[0] = weigh(s0, top0, own0)
        top_ref[0] = jnp.broadcast_to(top0, top_ref.shape[1:])
        s1 = scores(1, own1, own_mask(1))
        s2 = scores(1, own0, None)
        top1 = jnp.maximum(jnp.max(s1, axis=0, keepdims=True), jnp.max(s2, axis=0, keepdims=True))
        acc_ref[1] = weigh(s1, top1, own1) + weigh(s2, top1, own0)
        top_ref[1] = jnp.broadcast_to(top1, top_ref.shape[1:])

    def other():
        at = lax.rem(me + j, n)
        kind, mask = other_mask(at)
        is_prompt = kind == 0
        tile0, tile1 = kv_ref[at, 0, g], kv_ref[at, kind, g]
        s1 = scores(1, tile0, None)
        s2 = scores(kind, tile1, mask)
        old_p, old_c = top_ref[0, 0:1, :], top_ref[1, 0:1, :]
        high1 = jnp.max(s1, axis=0, keepdims=True)
        high2 = jnp.max(s2, axis=0, keepdims=True)
        top_p = jnp.where(is_prompt, jnp.maximum(old_p, high2), old_p)
        top_c = jnp.maximum(old_c, jnp.where(is_prompt, high1, jnp.maximum(high1, high2)))
        part1 = weigh(s1, top_c, tile0)
        part2 = weigh(s2, jnp.where(is_prompt, top_p, top_c), tile1)
        acc_ref[0] = acc_ref[0] * jnp.exp2((old_p - top_p) * LOG2E) + jnp.where(is_prompt, part2, 0.0)
        acc_ref[1] = (
            acc_ref[1] * jnp.exp2((old_c - top_c) * LOG2E) + part1 + jnp.where(is_prompt, 0.0, part2)
        )
        top_ref[0] = jnp.broadcast_to(top_p, top_ref.shape[1:])
        top_ref[1] = jnp.broadcast_to(top_c, top_ref.shape[1:])

    return own, other


def attend_close(g, top_ref, acc_ref, o_ref, lse_ref):
    for b in range(2):
        acc = acc_ref[b]
        total = acc[0:1, :]
        o_ref[g, b] = (acc / total).T
        lse_ref[g, b] = jnp.broadcast_to(top_ref[b, 0:1, :] * LOG2E + jnp.log2(total), lse_ref.shape[2:])


def attend_back_step(n, me, g, j, deal_ref, start_ref, q_ref, kv_ref, do_ref, lse_ref, delta_ref, dqt_ref, dkv_ref):
    block = kv_ref.shape[3]
    rows = q_ref.shape[2]
    own_mask, other_mask = attend_masks(n, deal_ref, start_ref, block, rows)

    def pair(kind, tile, mask):
        q = q_ref[g, kind]
        do = do_ref[g, kind]
        p = jnp.exp2(nt(tile, q) * LOG2E - lse_ref[g, kind, 0:1, :])
        if mask is not None:
            p = jnp.where(mask, p, 0.0)
        ds = (p * (nt(tile, do) - delta_ref[g, kind, 0:1, :])).astype(BF16)
        return nn(ds, q) + nn(p.astype(BF16), do), tn(tile, ds)

    def own():
        own0, own1 = kv_ref[me, 0, g], kv_ref[me, 1, g]
        d0, q0 = pair(0, own0, own_mask(0))
        d1, q1 = pair(1, own1, own_mask(1))
        d2, q2 = pair(1, own0, None)
        dkv_ref[me, g, 0] = (d0 + d2).astype(dkv_ref.dtype)
        dkv_ref[me, g, 1] = d1.astype(dkv_ref.dtype)
        dqt_ref[0] = q0
        dqt_ref[1] = q1 + q2

    def other():
        at = lax.rem(me + j, n)
        kind, mask = other_mask(at)
        is_prompt = kind == 0
        full, q_full = pair(1, kv_ref[at, 0, g], None)
        part, q_part = pair(kind, kv_ref[at, kind, g], mask)
        dkv_ref[at, g, 0] = (full + jnp.where(is_prompt, part, 0.0)).astype(dkv_ref.dtype)
        dkv_ref[at, g, 1] = jnp.where(is_prompt, 0.0, part).astype(dkv_ref.dtype)
        dqt_ref[0] = dqt_ref[0] + jnp.where(is_prompt, q_part, 0.0)
        dqt_ref[1] = dqt_ref[1] + q_full + jnp.where(is_prompt, 0.0, q_part)

    return own, other


def row_deltas(g, do_ref, o_ref, row_ref):
    ones = jnp.ones((8, LANES), F32)
    for b in range(2):
        row_ref[b] = lax.dot_general(
            ones, do_ref[g, b].astype(F32) * o_ref[g, b], (((1,), (1,)), ((), ())),
            precision=lax.Precision.HIGHEST, preferred_element_type=F32,
        )


def gain_row(gains_ref, which, fsdp, shard):
    return jnp.concatenate([gains_ref[i, which : which + 1, :shard] for i in range(fsdp)], axis=1)


def project(sizes, fsdp, x_ref, gains_ref, attn_ref, cos_ref, sin_ref, n1_ref, q_ref, kv_at):
    heads, kvh, block = sizes
    x = x_ref[...].astype(F32)
    normed = (x * rms_inverse(x) * gain_row(gains_ref, 0, fsdp, x.shape[1] // fsdp)).astype(BF16)
    n1_ref[...] = normed
    count = -(-(heads + 2 * kvh) * HD // LANES)
    raw = []
    for t in range(0, count, 2):
        some = range(t, min(t + 2, count))
        wide = nn(normed, lanes(attn_ref, some))
        raw += [wide[:, i * LANES : (i + 1) * LANES] for i in range(len(some))]
    store_projection(sizes, raw, cos_ref[...], sin_ref[...], q_ref, kv_at)


def front_kernel(
    sizes, n, fsdp, plans, deal_ref, lengths_ref, xt_ref, gains_in, turns_ref,
    wq_ref, wkt_ref, wvt_ref, wo_ref, wg_ref, wu_ref, wdt_ref, cott_ref,
    x_ref, cos_ref, sin_ref, n1_ref, q_ref, kv_out, lse_ref, gains_ref, attn_out,
    result_ref, gr_ref, do_ref, delta_ref, gain_ref, out_grad, ff_grad, down_grad,
    attn, ff, down, kv_all, o_ref, gains, start_ref, top_ref, acc_ref, cot_ref,
    resid_ref, n2_ref, product_ref, gg_ref, gu_ref, turned_ref, gn_ref, out_stage, ff_stage, down_stage,
    send, recv, kv_send, kv_recv, local, out_sem,
):
    heads, kvh, block = sizes
    me, z = lax.axis_index("ctx"), lax.axis_index("fsdp")
    shard = wq_ref.shape[0]
    rows = sub(z * shard, shard, 16)
    half = (heads + 2 * kvh) * HD % LANES
    main = wo_ref.shape[1] - half
    wo = wo_ref[...]
    tiles = pack_tiles([wq_ref[...], wkt_ref[...].T, wvt_ref[...].T, wo[:, main:], wo[:, :main]])
    for t, tile in enumerate(tiles):
        attn[t, rows, :] = tile
    gains[z] = gains_in[...]
    greet("z", fsdp)
    refs = {ATTN: attn, FF: ff, DOWN: down, "gains": gains}
    run = both_cores(lambda core: weight_stages(core, fsdp, plans[0], refs, send, recv))
    run_kv = both_cores(lambda core: kv_stages(core, plans[1], kv_all, kv_send, kv_recv))
    run("gains_out", ("over_z", ATTN))
    for t in range(ff.shape[1]):
        ff[0, t, rows, :] = wg_ref[:, t * LANES : (t + 1) * LANES]
        ff[1, t, rows, :] = wu_ref[:, t * LANES : (t + 1) * LANES]
    down_shard = wdt_ref.shape[1]
    down_rows = sub(z * down_shard, down_shard, 16)
    for t, tile in enumerate(pack_tiles([wdt_ref[...].T])):
        down[t, down_rows, :] = tile
    first, last = natural_blocks(deal_ref, me)
    flip = deal_ref[2 * me] > deal_ref[2 * me + 1]
    x_ref[...] = ordered(flip, xt_ref[...].T)
    cot_ref[...] = ordered(flip, cott_ref[...].T)
    row = lax.broadcasted_iota(jnp.int32, cos_ref.shape, 0)
    natural = jnp.where(row < block, first * block + row, (last - 1) * block + row)
    offset = natural - n * block
    position = jnp.where(offset < 0, natural, natural - segment_start(lengths_ref, offset))
    angle = position.astype(F32) * turns_ref[0:1, :]
    lane = lax.broadcasted_iota(jnp.int32, cos_ref.shape, 1)
    cos_ref[...] = jnp.cos(angle)
    sine = jnp.sin(angle)
    sin_ref[...] = jnp.where(lax.rem(lane, HD) < HD // 2, -sine, sine)
    start_ref[...] = first_keys(n, deal_ref, lengths_ref, block, start_ref.shape[1])
    run(("spread", ATTN), ("over_z", DOWN), ("over_z", FF), ("forward", ATTN))
    run(("pass_far", ATTN), ("pass_corner", ATTN))
    run(("finish", ATTN), "gains_in")
    project(
        sizes, fsdp, x_ref, gains, attn, cos_ref, sin_ref, n1_ref, q_ref,
        lambda b, g: kv_all.at[me, b, g],
    )
    run_kv("start", "forward")
    run(("spread", DOWN))
    run_kv("pass_on", "finish")
    gains_ref[...] = gains[...]
    outs = [pltpu.make_async_copy(attn, attn_out, local.at[0]), pltpu.make_async_copy(kv_all, kv_out, local.at[1])]
    for copy in outs:
        copy.start()
    schedule = {
        4: (("forward", DOWN),),
        10: (("spread", FF),),
        16: (("pass_far", DOWN), ("pass_corner", DOWN)),
        24: (("forward", FF),),
        30: (("finish", DOWN),),
        38: (("pass_far", FF),),
    }

    @pl.loop(0, kvh * n)
    def _(step):
        g, j = step // n, step % n
        for at, names in schedule.items():
            pl.when(step == at)(functools.partial(run, *names))
        own, other = attend_step(n, me, g, j, deal_ref, start_ref, q_ref, kv_all, top_ref, acc_ref)
        pl.when(j == 0)(own)
        pl.when(j > 0)(other)
        pl.when(j == n - 1)(lambda: attend_close(g, top_ref, acc_ref, o_ref, lse_ref))

    def quarter_ready(i):
        pl.when(i == 0)(lambda: run((FINISH, FF, 0)))
        pl.when(i == 1)(lambda: run((FINISH, FF, 1), (FINISH, FF, 2)))
        pl.when(i == 3)(lambda: run(("pass_corner", FF), (FINISH, FF, 3)))
        return lax.bitwise_xor(me // 2, i)

    feed_forward(
        sizes, fsdp, quarter_ready, lambda: None, x_ref, cot_ref, gains, attn, ff, down, o_ref,
        result_ref, gr_ref, do_ref, delta_ref, gain_ref, out_grad, ff_grad, down_grad,
        resid_ref, n2_ref, product_ref, gg_ref, gu_ref, turned_ref, gn_ref, out_stage, ff_stage, down_stage, out_sem,
    )
    run("drain")
    run_kv("drain")
    for copy in outs:
        copy.wait()


def head_columns(sizes, ref, low):
    heads, kvh, block = sizes
    share = heads // kvh
    return jnp.concatenate(
        [
            jnp.concatenate(
                [
                    ref[h // share, b, (h % share) * block : (h % share + 1) * block, low : low + HD]
                    for h in range(heads)
                ],
                axis=1,
            )
            for b in range(2)
        ],
        axis=0,
    )


def feed_forward(
    sizes, fsdp, quarter_ready, all_ready, x_ref, cot_ref, gains_ref, attn_ref, ff_ref, down_ref, o_ref,
    result_ref, gr_ref, do_ref, delta_ref, gain_ref, out_grad, ff_grad, down_grad,
    resid_ref, n2_ref, product_ref, gg_ref, gu_ref, turned_ref, gn_ref, out_stage, ff_stage, down_stage, sem,
):
    heads, kvh, block = sizes
    share = heads // kvh
    rows, width = x_ref.shape
    hidden = product_ref.shape[1]
    mixed = (heads + 2 * kvh) * HD // LANES
    half = (heads + 2 * kvh) * HD % LANES
    count = attn_ref.shape[0]
    down_tiles = down_ref.shape[0]
    gain = gain_row(gains_ref, 1, fsdp, width // fsdp)
    attended = head_columns(sizes, o_ref, HD).astype(BF16)
    pieces = []
    for t in range(mixed, count, 2):
        pieces.append(nn(attended, lanes(attn_ref, range(t, min(t + 2, count)))))
    branch = jnp.concatenate(pieces, axis=1)
    branch = jnp.concatenate([branch[:, LANES:], branch[:, half:LANES]], axis=1)
    resid = x_ref[...].astype(F32) + branch
    resid_ref[...] = resid
    n2_ref[...] = (resid * rms_inverse(resid) * gain).astype(BF16)
    pad = down_tiles * LANES - width
    wide = 2 * LANES
    per = ff_ref.shape[1] // 4

    @pl.loop(0, 4)
    def _(i):
        q = quarter_ready(i)
        cot_wide = jnp.concatenate([cot_ref[...], jnp.zeros((rows, pad), BF16)], axis=1)
        for low in range(0, per, 2):
            size = min(2, per - low)
            first = q * per + low
            at = pl.ds(pl.multiple_of(first * LANES, LANES), size * LANES)
            n2 = n2_ref[...]
            gate = nn(n2, jnp.concatenate([ff_ref[0, first + t] for t in range(size)], axis=1))
            upward = nn(n2, jnp.concatenate([ff_ref[1, first + t] for t in range(size)], axis=1))
            grad = nt(cot_wide, jnp.concatenate([down_ref[t, at, :] for t in range(down_tiles)], axis=1))
            sigma = 1.0 / (1.0 + jnp.exp(-gate))
            activated = gate * sigma
            product_ref[:, at] = (activated * upward).astype(BF16)
            gg_ref[:, at] = (grad * upward * (sigma + activated * (1.0 - sigma))).astype(BF16)
            gu_ref[:, at] = (grad * activated).astype(BF16)

    all_ready()
    for low in range(0, width, wide):
        size = min(wide, width - low)
        part = nt(gg_ref[...], lanes(ff_ref.at[0], range(hidden // LANES), slice(low, low + size)))
        part = part + nt(gu_ref[...], lanes(ff_ref.at[1], range(hidden // LANES), slice(low, low + size)))
        gn_ref[:, low : low + size] = part
    turned_ref[...] = n2_ref[...].T

    def ff_out(j):
        return pltpu.make_async_copy(ff_stage.at[j % 2], ff_grad.at[:, pl.ds(2 * j, 2)], sem.at[j % 2])

    def down_out(j):
        at = pl.ds(pl.multiple_of(j * wide, wide), wide)
        return pltpu.make_async_copy(down_stage.at[j % 2], down_grad.at[:, at], sem.at[2 + j % 2])

    @pl.loop(0, hidden // wide)
    def _(j):
        at = pl.ds(pl.multiple_of(j * wide, wide), wide)
        slot = lax.rem(j, 2)

        @pl.when(j >= 2)
        def _():
            ff_out(j - 2).wait()
            down_out(j - 2).wait()

        for c, grad_ref in enumerate((gg_ref, gu_ref)):
            part = nn(turned_ref[...], grad_ref[:, at]).astype(BF16)
            ff_stage[slot, c, 0] = part[:, :LANES]
            ff_stage[slot, c, 1] = part[:, LANES:]
        flipped = product_ref[:, at].T
        cot_wide = jnp.concatenate([cot_ref[...], jnp.zeros((rows, pad), BF16)], axis=1)
        part = nn(flipped, cot_wide).astype(BF16)
        for t in range(down_tiles):
            down_stage[slot, t] = part[:, t * LANES : (t + 1) * LANES]
        ff_out(j).start()
        down_out(j).start()

    grad_normed = gn_ref[...]
    resid = resid_ref[...]
    inverse = rms_inverse(resid)
    scaled = resid * inverse
    weighted = grad_normed * gain
    gain_ref[0:1, :] = jnp.sum(grad_normed * scaled, axis=0, keepdims=True)
    grad_resid = cot_ref[...].astype(F32) + inverse * (
        weighted - scaled * jnp.mean(weighted * scaled, axis=1, keepdims=True)
    )
    gr_ref[...] = grad_resid
    gb = grad_resid.astype(BF16)
    main = width - (LANES - half)
    lined = jnp.concatenate([jnp.zeros((rows, half), BF16), gb[:, main:], gb[:, :main]], axis=1)
    turned_ref[...] = head_columns(sizes, o_ref, HD).astype(BF16).T
    for t in range(0, count - mixed, 2):
        part = nn(turned_ref[...], lined[:, t * LANES : (t + 2) * LANES]).astype(BF16)
        out_stage[t] = part[:, :LANES]
        out_stage[t + 1] = part[:, LANES:]
    out_copy = pltpu.make_async_copy(out_stage, out_grad, sem.at[4])
    out_copy.start()
    grad_att = []
    for low in range(0, width, wide):
        size = min(wide, width - low)
        grad_att.append(
            nt(lined, lanes(attn_ref, range(mixed, count), slice(low, low + size))).astype(BF16)
        )
    grad_att = jnp.concatenate(grad_att, axis=1)
    zero = jnp.zeros((block, HD), BF16)
    for h in range(heads):
        for b in range(2):
            do_ref[h // share, b, (h % share) * block : (h % share + 1) * block, :] = jnp.concatenate(
                [zero, grad_att[b * block : (b + 1) * block, h * HD : (h + 1) * HD]], axis=1
            )
    for g in range(kvh):
        row_deltas(g, do_ref, o_ref, delta_ref.at[g])
    for t in range(0, down_tiles, 2):
        low, high = t * LANES, min((t + 2) * LANES, width)
        part = nn(product_ref[...], lanes(down_ref, (t, t + 1)))
        result_ref[:, low:high] = (resid_ref[:, low:high] + part[:, : high - low]).astype(BF16)
    last = hidden // wide
    for j in (last - 2, last - 1):
        ff_out(j).wait()
        down_out(j).wait()
    out_copy.wait()


def add_rows(out, terms, rows):
    def add(views):
        total = views[1][0:rows, :].astype(F32)
        for term in views[2:]:
            total = total + term[0:rows, :].astype(F32)
        views[0][0:rows, :] = total.astype(out.dtype)

    refs = [out] + list(terms)
    if len(out.shape) == 2:
        add(refs)
    else:

        @pl.loop(0, out.shape[0])
        def _(lead):
            add([r.at[lead] for r in refs])


def grad_stages(core, fsdp, plan, sources, held, got, outs, gain_refs, send, recv, local):
    links = Links(core, fsdp, send, recv, plan)
    z, chip = links.z, links.chip
    near, far = lax.bitwise_xor(chip, links.first), lax.bitwise_xor(chip, links.second)
    corner = lax.bitwise_xor(chip, 3)
    shards = {k: sources[k].shape[-2] // fsdp for k in PACKAGES}
    mine = {k: Share(k, core, shards[k]) for k in PACKAGES}
    twin = {k: Share(k, 1 - core, shards[k]) for k in PACKAGES}
    stages = {}

    def hold(k, d, q):
        if k in held:
            return held[k].at[d, q]
        return mine[k].at(sources[k], lax.bitwise_xor(z, d), q)

    def load(k, d, q):
        slot = (PACKAGES.index(k) * fsdp + d) * 4 + q
        return pltpu.make_async_copy(
            mine[k].at(sources[k], lax.bitwise_xor(z, d), q), hold(k, d, q), local.at[slot]
        )

    def begin(k, d):
        zi = lax.bitwise_xor(z, d)
        for q in range(4):
            links.send((k, CORE, d, q), CORE, twin[k].at(sources[k], zi, q), twin[k].buffer(got[k][0].at[d, q]))
            if k in held:
                load(k, d, q).start()

    def stage1(k, d):
        share = mine[k]
        for q in range(4):
            links.landed((k, CORE, d, q), share.buffer(got[k][0].at[d, q]))
            if k in held:
                load(k, d, q).wait()
            add_rows(hold(k, d, q), (hold(k, d, q), got[k][0].at[d, q]), share.rows)
        for i, q in enumerate((near, corner)):
            links.send((k, FIRST, d, i), FIRST, hold(k, d, q), share.buffer(got[k][1].at[d, i]))

    def stage2(k, d):
        share = mine[k]
        for i in range(2):
            links.landed((k, FIRST, d, i), share.buffer(got[k][1].at[d, i]))
        add_rows(hold(k, d, far), (hold(k, d, far), got[k][1].at[d, 1]), share.rows)
        links.send((k, SECOND, d), SECOND, hold(k, d, far), share.buffer(got[k][2].at[d]))

    def stage3(k, d):
        share = mine[k]
        links.landed((k, SECOND, d), share.buffer(got[k][2].at[d]))
        add_rows(hold(k, d, chip), (hold(k, d, chip), got[k][1].at[d, 0], got[k][2].at[d]), share.rows)
        if d > 0:
            links.send((k, "z", d), d, hold(k, d, chip), share.buffer(got[k][3].at[d - 1]))

    def out_copy(k):
        slot = len(PACKAGES) * fsdp * 4 + PACKAGES.index(k)
        return pltpu.make_async_copy(hold(k, 0, chip), mine[k].at(outs[k], 0, chip), local.at[slot])

    def close(k):
        share = mine[k]
        for d in range(1, fsdp):
            links.landed((k, "z", d), share.buffer(got[k][3].at[d - 1]))
        final = hold(k, 0, chip)
        add_rows(final, [final] + [got[k][3].at[d - 1] for d in range(1, fsdp)], share.rows)
        for hop in (FIRST, SECOND):
            links.send((k, "out", hop), hop, final, share.at(outs[k], 0, chip))
        links.send((k, "out core", 0), CORE, final, share.at(outs[k], 0, chip))
        out_copy(k).start()

    def close2(k):
        share = mine[k]
        links.landed((k, "out", FIRST), share.at(outs[k], 0, near))
        piece = share.at(outs[k], 0, near)
        links.send((k, "out", "corner"), SECOND, piece, piece)
        links.send((k, "out core", 1), CORE, piece, piece)
        piece = share.at(outs[k], 0, far)
        links.landed((k, "out", SECOND), piece)
        links.send((k, "out core", 2), CORE, piece, piece)

    def close3(k):
        piece = mine[k].at(outs[k], 0, corner)
        links.landed((k, "out", "corner"), piece)
        links.send((k, "out core", 3), CORE, piece, piece)

    def close4(k):
        for i, q in ((0, chip), (1, far), (2, near), (3, corner)):
            links.landed((k, "out core", i), twin[k].at(outs[k], 0, q))
        out_copy(k).wait()

    for k in PACKAGES:
        for fn in (begin, stage1, stage2, stage3):
            for d in range(fsdp):
                stages[fn.__name__, k, d] = functools.partial(fn, k, d)
        for fn in (close, close2, close3, close4):
            stages[fn.__name__, k] = functools.partial(fn, k)

    gain_sum, gain_got, gain_z, gain_out = gain_refs

    def gain_step(i):
        if i > 0:
            links.landed(("gain", i - 1), gain_got.at[i - 1])
            gain_sum[i] = gain_sum[i - 1] + gain_got[i - 1]
        if i < 3:
            links.send(("gain", i), (CORE, FIRST, SECOND)[i], gain_sum.at[i], gain_got.at[i])
        else:
            for d in range(1, fsdp):
                links.send(("gain z", d), d, gain_sum.at[3, lax.bitwise_xor(z, d)], gain_z.at[d - 1])

    def gain_close():
        total = gain_sum[3, z]
        for d in range(1, fsdp):
            links.landed(("gain z", d), gain_z.at[d - 1])
            total = total + gain_z[d - 1]
        gain_out[...] = total

    for i in range(4):
        stages["gain", i] = functools.partial(gain_step, i)
    stages["gain close"] = gain_close
    stages["drain"] = links.drain
    return stages


def kv_grad_stages(core, plan, parts, kv_sum, got0, got1, got2, send, recv):
    links = Links(core, 1, send, recv, plan)
    chip = links.chip
    near, far = lax.bitwise_xor(chip, links.first), lax.bitwise_xor(chip, links.second)
    corner = lax.bitwise_xor(chip, 3)
    rows = parts.shape[3]
    stages = {}

    def start(g):
        for q in range(4):
            links.send((0, g, q), CORE, parts.at[2 * q + 1 - core, g], got0.at[g, q])

    def stage1(g):
        for q in range(4):
            links.landed((0, g, q), got0.at[g, q])
            add_rows(got0.at[g, q], (parts.at[2 * q + core, g], got0.at[g, q]), rows)
        for i, q in enumerate((near, corner)):
            links.send((1, g, i), FIRST, got0.at[g, q], got1.at[g, i])

    def stage2(g):
        for i in range(2):
            links.landed((1, g, i), got1.at[g, i])
        add_rows(got0.at[g, far], (got0.at[g, far], got1.at[g, 1]), rows)
        links.send((2, g), SECOND, got0.at[g, far], got2.at[g])

    def stage3(g):
        links.landed((2, g), got2.at[g])
        add_rows(kv_sum.at[g], (got0.at[g, chip], got1.at[g, 0], got2.at[g]), rows)

    for g in range(parts.shape[1]):
        for i, fn in enumerate((start, stage1, stage2, stage3)):
            stages[i, g] = functools.partial(fn, g)
    stages["drain"] = links.drain
    return stages


def back_kernel(
    sizes, n, fsdp, plans, deal_ref, lengths_ref, q_ref, kv_in, do_ref, delta_ref, lse_ref,
    x_ref, n1_ref, gr_ref, gains_ref, gain_two_ref, cos_ref, sin_ref, attn_ref, out_grad_ref, ff_grad, down_grad,
    tg_ref, gain_out, attn_out, ff_out, down_out,
    start_ref, spill_ref, chunk_ref, dqt_ref, dq_ref, dkv_ref, kv_sum, kv_got0, kv_got1, kv_got2, gp_ref, gn_ref, turned_ref, attn_grad,
    ff_a, down_a, attn_0, ff_0, down_0, attn_1, ff_1, down_1, attn_2, ff_2, down_2, attn_3, ff_3, down_3,
    gain_sum, gain_got, gain_z, send, recv, kv_send, kv_recv, local, ahead_sem,
):
    heads, kvh, block = sizes
    share = heads // kvh
    me = lax.axis_index("ctx")
    width = x_ref.shape[1]
    rows = x_ref.shape[0]
    greet("z", fsdp)
    sources = {ATTN: attn_grad, FF: ff_grad, DOWN: down_grad}
    held = {FF: ff_a, DOWN: down_a}
    got = {ATTN: (attn_0, attn_1, attn_2, attn_3), FF: (ff_0, ff_1, ff_2, ff_3), DOWN: (down_0, down_1, down_2, down_3)}
    outs = {ATTN: attn_out, FF: ff_out, DOWN: down_out}
    run = both_cores(
        lambda core: grad_stages(
            core, fsdp, plans[0], sources, held, got, outs, (gain_sum, gain_got, gain_z, gain_out), send, recv, local
        )
    )
    run_kv = both_cores(
        lambda core: kv_grad_stages(core, plans[1], dkv_ref, kv_sum, kv_got0, kv_got1, kv_got2, kv_send, kv_recv)
    )
    start_ref[...] = first_keys(n, deal_ref, lengths_ref, block, start_ref.shape[1])
    order = [d for d in range(1, fsdp)] + [0]
    chunks = [(k, d) for k in (FF, DOWN) for d in order]
    steps = []
    for i in range(len(chunks) + 7):
        names = []
        if i + 1 < len(chunks):
            names.append(("begin",) + chunks[i + 1])
        if i < len(chunks):
            names.append(("stage1",) + chunks[i])
        if 1 <= i <= len(chunks):
            names.append(("stage2",) + chunks[i - 1])
        if 2 <= i <= len(chunks) + 1:
            names.append(("stage3",) + chunks[i - 2])
        for last, k in ((len(order) + 1, FF), (len(chunks) + 1, DOWN)):
            for extra, what in enumerate(("close", "close2", "close3", "close4")):
                if i == last + 1 + extra:
                    names.append((what, k))
        steps.append(names)
    run(("begin",) + chunks[0])
    width_tiles = -(-(heads + 2 * kvh) // 2)
    ahead = [
        pltpu.make_async_copy(out_grad_ref.at[0], spill_ref, ahead_sem.at[0]),
        pltpu.make_async_copy(
            out_grad_ref.at[pl.ds(1, attn_grad.shape[0] - width_tiles)],
            attn_grad.at[pl.ds(width_tiles, attn_grad.shape[0] - width_tiles)], ahead_sem.at[1],
        ),
    ]
    wide = 2 * LANES

    def weight_rows(i):
        size = min(wide, width - i * wide)
        return pltpu.make_async_copy(
            attn_ref.at[pl.ds(0, width_tiles), pl.ds(i * wide, size)],
            chunk_ref.at[i % 2, :, pl.ds(0, size)], ahead_sem.at[2 + i % 2],
        )

    for copy in ahead + [weight_rows(0), weight_rows(1)]:
        copy.start()
    total = kvh * n
    pace = 12
    kv_due = sorted((8 * (i + 1) + (0, 3, 11, 19)[stage], stage, i) for i in range(kvh) for stage in range(4))

    @pl.loop(0, total)
    def _(step):
        g, j = step // n, step % n
        for i, names in enumerate(steps):
            if i * pace < total:
                pl.when(step == i * pace)(functools.partial(run, *names))
        for due, stage, i in kv_due:
            if due < total:
                pl.when(step == due)(functools.partial(run_kv, (stage, i)))
        own, other = attend_back_step(
            n, me, g, j, deal_ref, start_ref, q_ref, kv_in, do_ref, lse_ref, delta_ref, dqt_ref, dkv_ref
        )
        pl.when(j == 0)(own)
        pl.when(j > 0)(other)

        @pl.when(j == n - 1)
        def _():
            dq_ref[g] = jnp.concatenate([(dqt_ref[b] * 0.125).T[:, :HD] for b in range(2)], axis=1)

    cos, sin = cos_ref[...], -sin_ref[...]

    def head(index):
        if index < heads:
            return jnp.concatenate(
                [
                    dq_ref[index // share, (index % share) * block : (index % share + 1) * block, b * HD : (b + 1) * HD]
                    for b in range(2)
                ],
                axis=0,
            )
        g = index - heads
        low = 0 if g < kvh else HD
        return jnp.concatenate([kv_sum[g % kvh, b, :, low : low + HD] for b in range(2)], axis=0)

    count = heads + 2 * kvh
    tiles = -(-count // 2)
    turned_ref[...] = n1_ref[...].T

    def some_tiles(low, high):
        for t in range(low, high):
            right = head(2 * t + 1) if 2 * t + 1 < count else jnp.zeros((rows, HD), F32)
            pair = jnp.concatenate([head(2 * t), right], axis=1)
            if 2 * t < heads + kvh:
                pair = rope_tile(pair, cos, sin)
            gp_ref[:, t * LANES : (t + 1) * LANES] = pair.astype(BF16)
        for t in range(low, high, 2):
            some = min(2, high - t)
            part = nn(turned_ref[...], gp_ref[:, t * LANES : (t + some) * LANES]).astype(BF16)
            for i in range(some):
                tile = part[:, i * LANES : (i + 1) * LANES]
                attn_grad[t + i] = tile + spill_ref[...] if t + i == tiles - 1 else tile

    rest = [names for i, names in enumerate(steps) if i * pace >= total]
    late = [(stage, i) for due, stage, i in kv_due if due >= total]
    run_kv(late[0])
    some_tiles(0, heads // 2)
    for copy in ahead:
        copy.wait()
    run_kv(*[key for key in late[1:] if key[0] < 2 or key[1] < kvh - 1])
    run(*rest[0])
    run_kv(*[key for key in late[1:] if key[0] >= 2 and key[1] == kvh - 1])
    some_tiles(heads // 2, tiles)
    run(("begin", ATTN, order[0]), ("begin", ATTN, order[1]), ("stage1", ATTN, order[0]), *rest[1])
    for i in range(-(-width // wide)):
        size = min(wide, width - i * wide)
        weight_rows(i).wait()
        rows_in = jnp.concatenate([chunk_ref[i % 2, t, 0:size, :] for t in range(tiles)], axis=1)
        gn_ref[:, i * wide : i * wide + size] = nt(gp_ref[...], rows_in)
        if (i + 2) * wide < width:
            weight_rows(i + 2).start()
    x = x_ref[...].astype(F32)
    inverse = rms_inverse(x)
    scaled = x * inverse
    grad_normed = gn_ref[...]
    weighted = grad_normed * gain_row(gains_ref, 0, fsdp, width // fsdp)
    gain_one = jnp.sum(grad_normed * scaled, axis=0, keepdims=True)
    gain_two = gain_two_ref[0:1, :]
    shard = width // fsdp
    tail = gain_sum.shape[3] - shard
    for i in range(fsdp):
        both = jnp.concatenate(
            [gain_one[:, i * shard : (i + 1) * shard], gain_two[:, i * shard : (i + 1) * shard]], axis=0
        )
        both = jnp.concatenate([both, jnp.zeros((2, tail), F32)], axis=1)
        gain_sum[0, i] = jnp.concatenate([both, jnp.zeros((6, gain_sum.shape[3]), F32)], axis=0)
    run(("gain", 0))
    tg_ref[...] = (
        gr_ref[...] + inverse * (weighted - scaled * jnp.mean(weighted * scaled, axis=1, keepdims=True))
    ).astype(BF16)
    chunk2 = [(ATTN, d) for d in order]
    for i in range(1, len(chunk2) + 2):
        names = []
        if i + 1 < len(chunk2):
            names.append(("begin",) + chunk2[i + 1])
        if i < len(chunk2):
            names.append(("stage1",) + chunk2[i])
        if i <= len(chunk2):
            names.append(("stage2",) + chunk2[i - 1])
        if i >= 2:
            names.append(("stage3",) + chunk2[i - 2])
        if i <= 3:
            names.append(("gain", i))
        if i + 1 < len(rest):
            names += rest[i + 1]
        run(*names)
    for i, what in enumerate(("close", "close2", "close3", "close4")):
        names = rest[len(chunk2) + 3 + i] if len(chunk2) + 3 + i < len(rest) else []
        run((what, ATTN), *names)
    for names in rest[len(chunk2) + 7 :]:
        run(*names)
    run("gain close", "drain")
    run_kv("drain")


def whole(shape, dtype):
    return jax.ShapeDtypeStruct(shape, dtype)


def params(ident=None):
    extra = {} if ident is None else {"collective_id": ident, "has_side_effects": True}
    return pltpu.CompilerParams(vmem_limit_bytes=VMEM_LIMIT, **extra)


SMEM = pl.BlockSpec(memory_space=pltpu.SMEM)
VMEM = pl.BlockSpec(memory_space=pltpu.VMEM)
ANY = pl.BlockSpec(memory_space=pl.ANY)


def finish_kernel(
    heads, deal_ref, result_ref, tokens_ref, attn_ref, ff_ref, down_ref,
    out_ref, tg_ref, q_ref, kt_ref, vt_ref, o_ref, gate_ref, up_ref, dt_ref,
):
    me = lax.axis_index("ctx")
    flip = deal_ref[2 * me] > deal_ref[2 * me + 1]
    out_ref[...] = ordered(flip, result_ref[...]).T
    tg_ref[...] = ordered(flip, tokens_ref[...]).T
    width, kv_width = q_ref.shape[1], kt_ref.shape[0]
    half = width % LANES
    full = width // LANES

    def tile(t):
        return attn_ref[t].astype(F32)

    for t in range(full):
        q_ref[:, t * LANES : (t + 1) * LANES] = tile(t)
    q_ref[:, full * LANES :] = tile(full)[:, :half]
    kt_ref[0 : LANES - half, :] = tile(full).T[half:, :]
    at = LANES - half
    for t in range(full + 1, (width + kv_width) // LANES):
        kt_ref[at : at + LANES, :] = tile(t).T
        at += LANES
    first = (width + kv_width) // LANES
    spill = (width + 2 * kv_width) // LANES
    for i in range(spill - first):
        vt_ref[i * LANES : (i + 1) * LANES, :] = tile(first + i).T
    vt_ref[(spill - first) * LANES :, :] = tile(spill).T[: kv_width % LANES, :]
    for i in range(full):
        o_ref[:, i * LANES : (i + 1) * LANES] = tile(spill + 1 + i)
    o_ref[:, full * LANES :] = tile(spill)[:, LANES - half :]
    for t in range(ff_ref.shape[1]):
        gate_ref[:, t * LANES : (t + 1) * LANES] = ff_ref[0, t].astype(F32)
        up_ref[:, t * LANES : (t + 1) * LANES] = ff_ref[1, t].astype(F32)
    for t in range(down_ref.shape[0]):
        high = min((t + 1) * LANES, dt_ref.shape[0])
        dt_ref[t * LANES : high, :] = down_ref[t].astype(F32).T[: high - t * LANES, :]


def cube_body(
    tokens, attn_gain, query_weight, key_weight, value_weight, out_weight, mlp_gain, gate_weight,
    up_weight, down_weight, cotangent, cont_lengths, block_deal,
):
    n, fsdp = lax.axis_size("ctx"), lax.axis_size("fsdp")
    me = lax.axis_index("ctx")
    row_count, width = tokens.shape[1:]
    kv_width = key_weight.shape[1]
    shard, hidden = gate_weight.shape
    down_shard = down_weight.shape[0]
    block = row_count // 2
    heads, kvh = width // HD, kv_width // HD
    share = heads // kvh
    stack = share * block
    sizes = (heads, kvh, block)
    half_turns = THETA ** (-2.0 * jnp.arange(HD // 2, dtype=F32) / HD)
    turns = jnp.tile(half_turns, (8, LANES // (HD // 2)))
    pad = -shard % LANES
    gains_in = jnp.pad(jnp.stack([attn_gain, mlp_gain]).astype(F32), ((0, 6), (0, pad)))
    gain_shape = (fsdp,) + gains_in.shape
    attn_tiles = (2 * width + 2 * kv_width) // LANES
    ff_tiles = hidden // LANES
    down_tiles = -(-width // LANES)
    heads_shape = (kvh, 2, stack, LANES)
    row_shape = (kvh, 2, 8, stack)
    kv_shape = (n, 2, kvh, block, LANES)
    dma = pltpu.SemaphoreType.DMA
    mixed = (width + 2 * kv_width) // LANES
    wide = 2 * LANES
    (
        x, cos, sin, normed_one, q, kv_all, lse, gains, w_attn,
        result, grad_resid, grad_heads, deltas, gain_two, out_grad, ff_grad, down_grad,
    ) = pl.pallas_call(
        functools.partial(front_kernel, sizes, n, fsdp, ({}, {})),
        out_shape=(
            whole((row_count, width), BF16),
            whole((row_count, LANES), F32),
            whole((row_count, LANES), F32),
            whole((row_count, width), BF16),
            whole(heads_shape, BF16),
            whole(kv_shape, BF16),
            whole(row_shape, F32),
            whole(gain_shape, F32),
            whole((attn_tiles, fsdp * shard, LANES), BF16),
            whole((row_count, width), BF16),
            whole((row_count, width), F32),
            whole(heads_shape, BF16),
            whole(row_shape, F32),
            whole((8, width), F32),
            whole((attn_tiles - mixed, width, LANES), BF16),
            whole((2, ff_tiles, width, LANES), BF16),
            whole((down_tiles, hidden, LANES), BF16),
        ),
        in_specs=[SMEM] * 2 + [VMEM] * 11,
        out_specs=(VMEM,) * 5 + (ANY, VMEM, VMEM, ANY) + (VMEM,) * 5 + (ANY,) * 3,
        scratch_shapes=[
            pltpu.VMEM((attn_tiles, fsdp * shard, LANES), BF16),
            pltpu.VMEM((2, ff_tiles, fsdp * shard, LANES), BF16),
            pltpu.VMEM((down_tiles, fsdp * down_shard, LANES), BF16),
            pltpu.VMEM(kv_shape, BF16),
            pltpu.VMEM(heads_shape, F32),
            pltpu.VMEM(gain_shape, F32),
            pltpu.VMEM((8, stack), jnp.int32),
            pltpu.VMEM((2, 8, stack), F32),
            pltpu.VMEM((2, LANES, stack), F32),
            pltpu.VMEM((row_count, width), BF16),
            pltpu.VMEM((row_count, width), F32),
            pltpu.VMEM((row_count, width), BF16),
            pltpu.VMEM((row_count, hidden), BF16),
            pltpu.VMEM((row_count, hidden), BF16),
            pltpu.VMEM((row_count, hidden), BF16),
            pltpu.VMEM((width, row_count), BF16),
            pltpu.VMEM((row_count, width), F32),
            pltpu.VMEM((attn_tiles - mixed, width, LANES), BF16),
            pltpu.VMEM((2, 2, 2, width, LANES), BF16),
            pltpu.VMEM((2, down_tiles, wide, LANES), BF16),
            dma((75,)), dma((75,)), dma((14,)), dma((14,)), dma((2,)), dma((5,)),
        ],
        compiler_params=params(0),
        name="front",
    )(
        block_deal, cont_lengths, tokens[0].T, gains_in, turns,
        query_weight, key_weight.T, value_weight.T, out_weight, gate_weight, up_weight, down_weight.T,
        cotangent[0].T,
    )

    attn_rows = -(-shard // 32) * 16
    shapes = ((attn_tiles // 4, attn_rows, LANES), (ff_tiles // 4, shard, LANES), (down_shard, LANES))
    buffers = [pltpu.VMEM((fsdp, 4) + shape, BF16) for shape in shapes[1:]]
    for lead in ((fsdp, 4), (fsdp, 2), (fsdp,), (fsdp - 1,)):
        buffers += [pltpu.VMEM(lead + shape, BF16) for shape in shapes]
    qkv_tiles = -(-(width + 2 * kv_width) // LANES)
    piece = (2, block, LANES)
    tokens_grad, gain_grads, attn_w, ff_w, down_w = pl.pallas_call(
        functools.partial(back_kernel, sizes, n, fsdp, ({}, {})),
        out_shape=(
            whole((row_count, width), BF16),
            whole(gains_in.shape, F32),
            whole((attn_tiles, shard, LANES), BF16),
            whole((2, ff_tiles, shard, LANES), BF16),
            whole((down_tiles, down_shard, LANES), BF16),
        ),
        in_specs=[SMEM] * 2 + [VMEM] * 12 + [ANY] * 4,
        out_specs=(VMEM, VMEM, ANY, ANY, ANY),
        scratch_shapes=[
            pltpu.VMEM((8, stack), jnp.int32),
            pltpu.VMEM((width, LANES), BF16),
            pltpu.VMEM((2, qkv_tiles, 2 * LANES, LANES), BF16),
            pltpu.VMEM((2, LANES, stack), F32),
            pltpu.VMEM((kvh, stack, LANES), F32),
            pltpu.VMEM((n, kvh) + piece, BF16),
            pltpu.VMEM((kvh,) + piece, F32),
            pltpu.VMEM((kvh, 4) + piece, BF16),
            pltpu.VMEM((kvh, 2) + piece, BF16),
            pltpu.VMEM((kvh,) + piece, BF16),
            pltpu.VMEM((row_count, qkv_tiles * LANES), BF16),
            pltpu.VMEM((row_count, width), F32),
            pltpu.VMEM((width, row_count), BF16),
            pltpu.VMEM((attn_tiles, width, LANES), BF16),
        ]
        + buffers
        + [
            pltpu.VMEM((4,) + gain_shape, F32),
            pltpu.VMEM((3,) + gain_shape, F32),
            pltpu.VMEM((fsdp - 1,) + gains_in.shape, F32),
            dma((120,)), dma((120,)), dma((7 * kvh,)), dma((7 * kvh,)), dma((51,)), dma((4,)),
        ],
        compiler_params=params(1),
        name="back",
    )(
        block_deal, cont_lengths, q, kv_all, grad_heads, deltas, lse, x, normed_one, grad_resid, gains, gain_two,
        cos, sin, w_attn, out_grad, ff_grad, down_grad,
    )

    out_t, tg_t, q_w, k_t, v_t, o_w, gate_w, up_w, d_t = pl.pallas_call(
        functools.partial(finish_kernel, heads),
        out_shape=(
            whole((width, row_count), BF16),
            whole((width, row_count), BF16),
            whole((shard, width), F32),
            whole((kv_width, shard), F32),
            whole((kv_width, shard), F32),
            whole((shard, width), F32),
            whole((shard, hidden), F32),
            whole((shard, hidden), F32),
            whole((width, down_shard), F32),
        ),
        in_specs=[SMEM] + [VMEM] * 5,
        out_specs=(VMEM,) * 9,
        compiler_params=params(),
        name="finish",
    )(block_deal, result, tokens_grad, attn_w, ff_w, down_w)
    return (
        out_t.T[None],
        tg_t.T[None],
        gain_grads[0, :shard],
        q_w,
        k_t.T,
        v_t.T,
        o_w,
        gain_grads[1, :shard],
        gate_w,
        up_w,
        d_t.T,
    )


def head_of(tiles, index):
    start = (index % 2) * HD
    return tiles[index // 2][:, start : start + HD]


def project_kernel(sizes, x_ref, gain_ref, w_ref, cos_ref, sin_ref, n1_ref, q_ref, kv_ref):
    heads, kvh, block = sizes
    share = heads // kvh
    x = x_ref[...].astype(F32)
    inverse = lax.rsqrt(jnp.mean(x * x, axis=1, keepdims=True) + EPSILON)
    normed = (x * inverse * gain_ref[...]).astype(BF16)
    n1_ref[...] = normed
    width = (heads + 2 * kvh) * HD
    raw = nn(normed, w_ref[:, :width])
    cos = cos_ref[...]
    sin = sin_ref[...]
    tiles = []
    for j in range((heads + kvh) * HD // LANES):
        tiles.append(rope_tile(raw[:, j * LANES : (j + 1) * LANES], cos, sin).astype(BF16))
    zero = jnp.zeros((block, HD), BF16)
    for h in range(heads):
        piece = head_of(tiles, h) * jnp.asarray(0.125, BF16)
        g, i = h // share, h % share
        for b in range(2):
            q_ref[g, b, i * block : (i + 1) * block, :] = jnp.concatenate(
                [piece[b * block : (b + 1) * block], zero], axis=1
            )
    for g in range(kvh):
        start = (heads + kvh + g) * HD
        value = raw[:, start : start + HD].astype(BF16)
        pair = jnp.concatenate([head_of(tiles, heads + g), value], axis=1)
        for b in range(2):
            kv_ref[b, :, g * LANES : (g + 1) * LANES] = pair[b * block : (b + 1) * block]


def attend_kernel(
    n, me_ref, pick_ref, segq_ref, segk_ref, q_ref, kv_ref, o_ref, lse_ref, s1_ref, p1_ref, s2_ref, p2_ref
):
    me = me_ref[0]
    block = kv_ref.shape[2]
    rows = q_ref.shape[2]
    keys = n * block
    qc = q_ref[0, 1]
    prompt = kv_ref[:, 0].reshape(keys, LANES)
    s1_ref[...] = nt(qc, prompt)
    own = []
    for b in range(2):
        s2_ref[b] = nt(q_ref[0, b], kv_ref[me, b])
    for j in range(1, n):
        at = lax.rem(me + j, n)
        kind = pick_ref[j]
        s2_ref[j + 1] = nt(q_ref[0, kind], kv_ref[at, kind])
    step = 16
    kinds = [pick_ref[j] == 0 for j in range(n)]

    def fold(s):
        return jnp.maximum(
            s[:, :LANES],
            jnp.concatenate(
                [s[:, LANES:], jnp.full((step, 2 * LANES - block), MASKED, F32)], axis=1
            ),
        )

    def chunk(at, carry):
        r = pl.multiple_of(at * step, step)
        rs = pl.ds(r, step)
        in_block = lax.rem(r, block)
        tri = lax.broadcasted_iota(jnp.int32, (step, block), 1) <= (
            in_block + lax.broadcasted_iota(jnp.int32, (step, block), 0)
        )
        segq = segq_ref[rs, :]
        s1 = s1_ref[rs, :]
        top_c = s1[:, :LANES]
        for t in range(1, keys // LANES):
            top_c = jnp.maximum(top_c, s1[:, t * LANES : (t + 1) * LANES])
        dp = jnp.where(tri, s2_ref[0, rs, :], MASKED)
        dc = jnp.where(tri & (segq == segk_ref[0]), s2_ref[1, rs, :], MASKED)
        top_c = jnp.maximum(top_c, fold(dc))
        top_p = fold(dp)
        others = []
        for j in range(1, n):
            s = jnp.where((segq == segk_ref[j]) | kinds[j], s2_ref[j + 1, rs, :], MASKED)
            others.append(s)
            f = fold(s)
            top_p = jnp.maximum(top_p, jnp.where(kinds[j], f, MASKED))
            top_c = jnp.maximum(top_c, jnp.where(kinds[j], MASKED, f))
        m_p = jnp.max(top_p, axis=1, keepdims=True)
        m_c = jnp.max(top_c, axis=1, keepdims=True)
        p1_ref[rs, :] = jnp.exp2((s1 - m_c) * LOG2E).astype(BF16)
        p2_ref[0, rs, :] = jnp.exp2((dp - m_p) * LOG2E).astype(BF16)
        p2_ref[1, rs, :] = jnp.exp2((dc - m_c) * LOG2E).astype(BF16)
        for j in range(1, n):
            m = jnp.where(kinds[j], m_p, m_c)
            p2_ref[j + 1, rs, :] = jnp.exp2((others[j - 1] - m) * LOG2E).astype(BF16)
        lse_ref[0, 0, rs, :] = jnp.broadcast_to(m_p * LOG2E, (step, LANES))
        lse_ref[0, 1, rs, :] = jnp.broadcast_to(m_c * LOG2E, (step, LANES))
        return carry

    lax.fori_loop(0, rows // step, chunk, 0)

    def with_ones(tile):
        return jnp.concatenate([tile, jnp.ones(tile.shape, BF16)], axis=1)

    acc = [nn(p2_ref[b], with_ones(kv_ref[me, b])) for b in range(2)]
    acc[1] = acc[1] + nn(p1_ref[...], with_ones(prompt))
    for j in range(1, n):
        at = lax.rem(me + j, n)
        part = nn(p2_ref[j + 1], with_ones(kv_ref[at, pick_ref[j]]))
        acc[0] = acc[0] + jnp.where(kinds[j], part, 0.0)
        acc[1] = acc[1] + jnp.where(kinds[j], 0.0, part)
    for b in range(2):
        total = acc[b][:, LANES:]
        o_ref[0, b] = acc[b][:, :LANES] / total
        lse_ref[0, b] = lse_ref[0, b] + jnp.log2(total)


def attend_back_kernel(
    n, me_ref, pick_ref, segq_ref, segk_ref, q_ref, kv_ref, do_ref, o_ref, lse_ref, dq_ref, dkv_ref, row_ref, dqt_ref
):
    me = me_ref[0]
    block = kv_ref.shape[2]
    rows = q_ref.shape[2]
    first = (lax.broadcasted_iota(jnp.int32, (8, LANES), 1) == 0).astype(F32)
    ones = jnp.ones((8, LANES), F32)

    def to_row(lhs, matrix):
        return lax.dot_general(
            lhs, matrix, (((1,), (1,)), ((), ())), precision=lax.Precision.HIGHEST,
            preferred_element_type=F32,
        )

    for b in range(2):
        row_ref[b] = to_row(first, lse_ref[0, b])
        row_ref[2 + b] = to_row(ones, do_ref[0, b].astype(F32) * o_ref[0, b])
    lane_rows = lax.rem(lax.broadcasted_iota(jnp.int32, (block, rows), 1), block)
    tri = lax.broadcasted_iota(jnp.int32, (block, rows), 0) <= lane_rows

    def pair(kind, tile, mask):
        q = q_ref[0, kind]
        do = do_ref[0, kind]
        p = jnp.exp2(nt(tile, q) * LOG2E - row_ref[kind, 0:1, :])
        if mask is not None:
            p = jnp.where(mask, p, 0.0)
        ds = (p * (nt(tile, do) - row_ref[2 + kind, 0:1, :])).astype(BF16)
        return nn(ds, q) + nn(p.astype(BF16), do), tn(tile, ds)

    segq = segq_ref[0:1, :]
    same_own = segq == segk_ref[0]
    own0, own1 = kv_ref[me, 0], kv_ref[me, 1]
    d0, q0 = pair(0, own0, tri)
    d1, q1 = pair(1, own1, tri & same_own)
    d2, q2 = pair(1, own0, None)
    dkv_ref[me, 0] = (d0 + d2).astype(dkv_ref.dtype)
    dkv_ref[me, 1] = d1.astype(dkv_ref.dtype)
    dqt_ref[0] = q0
    dqt_ref[1] = q1 + q2

    def other(j, carry):
        at = lax.rem(me + j, n)
        kind = pick_ref[j]
        is_prompt = kind == 0
        full, q_full = pair(1, kv_ref[at, 0], None)
        mask = (segq == segk_ref[j]) | is_prompt
        part, q_part = pair(kind, kv_ref[at, kind], mask)
        dkv_ref[at, 0] = (full + jnp.where(is_prompt, part, 0.0)).astype(dkv_ref.dtype)
        dkv_ref[at, 1] = jnp.where(is_prompt, 0.0, part).astype(dkv_ref.dtype)
        dqt_ref[0] = dqt_ref[0] + jnp.where(is_prompt, q_part, 0.0)
        dqt_ref[1] = dqt_ref[1] + q_full + jnp.where(is_prompt, 0.0, q_part)
        return carry

    lax.fori_loop(1, n, other, 0)
    for b in range(2):
        dq_ref[0, b] = (dqt_ref[b] * 0.125).T


def mid_kernel(sizes, o_ref, x_ref, wo_ref, gain_ref, att_ref, resid_ref, n2_ref):
    heads, kvh, block = sizes
    share = heads // kvh
    for b in range(2):
        columns = []
        for h in range(heads):
            g, i = h // share, h % share
            columns.append(o_ref[g, b, i * block : (i + 1) * block, HD:])
        attended = jnp.concatenate(columns, axis=1).astype(BF16)
        rs = slice(b * block, (b + 1) * block)
        att_ref[rs, :] = attended
        resid = x_ref[rs, :].astype(F32) + nn(attended, wo_ref[...])
        resid_ref[rs, :] = resid
        inverse = lax.rsqrt(jnp.mean(resid * resid, axis=1, keepdims=True) + EPSILON)
        n2_ref[rs, :] = (resid * inverse * gain_ref[...]).astype(BF16)


def branch_kernel(sizes, gb_ref, wo_ref, do_ref):
    heads, kvh, block = sizes
    share = heads // kvh
    grad = nt(gb_ref[...], wo_ref[...]).astype(BF16)
    zero = jnp.zeros((block, HD), BF16)
    for h in range(heads):
        g, i = h // share, h % share
        for b in range(2):
            do_ref[g, b, i * block : (i + 1) * block, :] = jnp.concatenate(
                [zero, grad[b * block : (b + 1) * block, h * HD : (h + 1) * HD]], axis=1
            )


def unrope_kernel(sizes, dq_ref, dkv_ref, cos_ref, sin_ref, out_ref):
    heads, kvh, block = sizes
    share = heads // kvh
    for b in range(2):
        rs = slice(b * block, (b + 1) * block)
        cos, sin = cos_ref[rs, :], -sin_ref[rs, :]
        columns = [
            dq_ref[h // share, b, (h % share) * block : (h % share + 1) * block, :HD]
            for h in range(heads)
        ]
        columns += [dkv_ref[b, :, g * LANES : g * LANES + HD].astype(F32) for g in range(kvh)]
        tiles = []
        for j in range((heads + kvh) // 2):
            pair = jnp.concatenate(columns[2 * j : 2 * j + 2], axis=1)
            tiles.append(rope_tile(pair, cos, sin).astype(BF16))
        values = [dkv_ref[b, :, g * LANES + HD : (g + 1) * LANES].astype(BF16) for g in range(kvh)]
        out_ref[rs, :] = jnp.concatenate(tiles + values, axis=1)


def local_call(kernel, out_shape, name, **extra):
    return pl.pallas_call(
        kernel,
        out_shape=out_shape,
        compiler_params=pltpu.CompilerParams(vmem_limit_bytes=VMEM_LIMIT),
        name=name,
        **extra,
    )


def gather_rows(array, axis):
    return lax.all_gather(array, axis, axis=0, tiled=True)


def norm_back(grad_normed, scaled, inverse, gain):
    weighted = grad_normed * gain
    return inverse * (weighted - scaled * jnp.mean(weighted * scaled, axis=1, keepdims=True))


def general_body(
    tokens, attn_gain, query_weight, key_weight, value_weight, out_weight, mlp_gain, gate_weight,
    up_weight, down_weight, cotangent, cont_lengths, block_deal,
):
    n = lax.axis_size("ctx")
    me = lax.axis_index("ctx")
    row_count, width = tokens.shape[1:]
    kv_width = key_weight.shape[1]
    hidden = gate_weight.shape[1]
    block = row_count // 2
    total_rows = row_count * n
    prompt_size = total_rows // 2
    heads, kvh = width // HD, kv_width // HD
    share = heads // kvh
    stack = share * block
    sizes = (heads, kvh, block)

    deal = block_deal.reshape(n, 2)
    flip = deal[me, 0] > deal[me, 1]

    def ordered(rows):
        halves = rows.reshape(2, block, rows.shape[-1])
        return jnp.where(flip, halves[::-1], halves).reshape(rows.shape)

    x = ordered(tokens[0])
    cot = ordered(cotangent[0])
    naturals = jnp.sort(deal, axis=1)
    natural = naturals[:, :, None] * block + jnp.arange(block, dtype=jnp.int32)
    offset = natural - prompt_size
    lengths = cont_lengths[0]
    ending = jnp.cumsum(lengths)
    segment = jnp.sum((offset[..., None] >= ending).astype(jnp.int32), axis=-1)
    inside = segment[..., None] == jnp.arange(lengths.shape[0], dtype=jnp.int32)
    beginning = jnp.sum(jnp.where(inside, ending - lengths, 0), axis=-1)
    position = jnp.where(offset < 0, natural, prompt_size + offset - beginning)
    own_position = position[me].reshape(row_count)
    frequency = THETA ** (-2.0 * jnp.arange(HD // 2, dtype=F32) / HD)
    angle = own_position.astype(F32)[:, None] * frequency[None, :]
    cos, sin = jnp.cos(angle), jnp.sin(angle)
    cos = jnp.concatenate([cos, cos, cos, cos], axis=1)
    sin = jnp.concatenate([-sin, sin, -sin, sin], axis=1)
    around = (me + jnp.arange(n, dtype=jnp.int32)) % n
    first_natural = naturals[:, 0]
    pick = (first_natural[around] >= first_natural[me]).astype(jnp.int32)
    segk = segment[around, 1]
    segq = jnp.tile(segment[me, 1], share)
    me_arr = me.reshape(1).astype(jnp.int32)

    attn_rows = jnp.concatenate([query_weight, key_weight, value_weight, out_weight], axis=1)
    w_attn = gather_rows(attn_rows, "fsdp")
    qkv_width = width + 2 * kv_width
    w_qkv = w_attn[:, :qkv_width]
    w_out = w_attn[:, qkv_width:]
    gain_one = gather_rows(attn_gain, "fsdp").astype(F32)
    gain_two = gather_rows(mlp_gain, "fsdp").astype(F32)
    w_gate = gather_rows(gate_weight, "fsdp")
    w_up = gather_rows(up_weight, "fsdp")
    w_down = gather_rows(down_weight, "fsdp")

    normed_one, q, kv = local_call(
        functools.partial(project_kernel, sizes),
        (
            whole((row_count, width), BF16),
            whole((kvh, 2, stack, LANES), BF16),
            whole((2, block, kvh * LANES), BF16),
        ),
        "project",
    )(x, gain_one[None], w_attn, cos, sin)
    kv_all = lax.all_gather(kv, "ctx", axis=0)

    smem = pl.BlockSpec(memory_space=pltpu.SMEM)
    per_group = pl.BlockSpec((1, 2, stack, LANES), lambda g: (g, 0, 0, 0))
    kv_spec = pl.BlockSpec((n, 2, block, LANES), lambda g: (0, 0, 0, g))

    def full(array):
        rank = array.ndim
        return pl.BlockSpec(array.shape, lambda g: (0,) * rank)

    segq_col, segk_row = segq[:, None], segk[:, None, :]
    attended_heads, lse = local_call(
        functools.partial(attend_kernel, n),
        (whole((kvh, 2, stack, LANES), F32), whole((kvh, 2, stack, LANES), F32)),
        "attend",
        grid=(kvh,),
        in_specs=[smem, smem, full(segq_col), full(segk_row), per_group, kv_spec],
        out_specs=(per_group, per_group),
        scratch_shapes=[
            pltpu.VMEM((stack, n * block), F32),
            pltpu.VMEM((stack, n * block), BF16),
            pltpu.VMEM((n + 1, stack, block), F32),
            pltpu.VMEM((n + 1, stack, block), BF16),
        ],
    )(me_arr, pick, segq_col, segk_row, q, kv_all)

    attended, resid, normed_two = local_call(
        functools.partial(mid_kernel, sizes),
        (
            whole((row_count, width), BF16),
            whole((row_count, width), F32),
            whole((row_count, width), BF16),
        ),
        "mid",
    )(attended_heads, x, w_out, gain_two[None])

    inverse_two = lax.rsqrt(jnp.mean(resid * resid, axis=1, keepdims=True) + EPSILON)
    scaled_two = resid * inverse_two
    gate = nn(normed_two, w_gate)
    upward = nn(normed_two, w_up)
    sigma = jax.nn.sigmoid(gate)
    activated = gate * sigma
    product = (activated * upward).astype(BF16)
    result = resid + nn(product, w_down)
    grad_prod = nt(cot, w_down)
    grad_gate = (grad_prod * upward * sigma * (1.0 + gate * (1.0 - sigma))).astype(BF16)
    grad_up = (grad_prod * activated).astype(BF16)
    grad_normed_two = nt(grad_gate, w_gate) + nt(grad_up, w_up)
    gain_two_part = jnp.sum(grad_normed_two * scaled_two, axis=0)
    grad_resid = cot.astype(F32) + norm_back(grad_normed_two, scaled_two, inverse_two, gain_two)
    grad_branch = grad_resid.astype(BF16)

    grad_heads = local_call(
        functools.partial(branch_kernel, sizes), whole((kvh, 2, stack, LANES), BF16), "branch"
    )(grad_branch, w_out)

    segq_row, segk_col = segq[None, :], segk[:, :, None]
    grad_query, grad_kv = local_call(
        functools.partial(attend_back_kernel, n),
        (whole((kvh, 2, stack, LANES), F32), whole((n, 2, block, kvh * LANES), F32)),
        "attend_back",
        grid=(kvh,),
        in_specs=[smem, smem, full(segq_row), full(segk_col)]
        + [per_group, kv_spec, per_group, per_group, per_group],
        out_specs=(per_group, kv_spec),
        scratch_shapes=[
            pltpu.VMEM((4, 8, stack), F32),
            pltpu.VMEM((2, LANES, stack), F32),
        ],
    )(me_arr, pick, segq_row, segk_col, q, kv_all, grad_heads, attended_heads, lse)

    kv_sum = lax.psum_scatter(grad_kv, "ctx", scatter_dimension=0, tiled=False)
    grad_projected = local_call(
        functools.partial(unrope_kernel, sizes), whole((row_count, qkv_width), BF16), "unrope"
    )(grad_query, kv_sum, cos, sin)

    x_float = x.astype(F32)
    inverse_one = lax.rsqrt(jnp.mean(x_float * x_float, axis=1, keepdims=True) + EPSILON)
    scaled_one = x_float * inverse_one
    grad_normed_one = nt(grad_projected, w_qkv)
    gain_one_part = jnp.sum(grad_normed_one * scaled_one, axis=0)
    tokens_grad = (
        grad_resid + norm_back(grad_normed_one, scaled_one, inverse_one, gain_one)
    ).astype(BF16)

    def spread(partial):
        rows = lax.psum_scatter(partial.astype(BF16), "fsdp", scatter_dimension=0, tiled=True)
        return lax.psum(rows, "ctx").astype(F32)

    grad_gate_w = spread(tn(normed_two, grad_gate))
    grad_up_w = spread(tn(normed_two, grad_up))
    grad_down_w = spread(tn(product, cot))
    grad_out_w = spread(tn(attended, grad_branch))
    grad_qkv_w = spread(tn(normed_one, grad_projected))
    gains = spread(jnp.stack([gain_one_part, gain_two_part], axis=1))
    return (
        ordered(result.astype(BF16))[None],
        ordered(tokens_grad)[None],
        gains[:, 0],
        grad_qkv_w[:, :width],
        grad_qkv_w[:, width : width + kv_width],
        grad_qkv_w[:, width + kv_width :],
        grad_out_w,
        gains[:, 1],
        grad_gate_w,
        grad_up_w,
        grad_down_w,
    )


def solution(mesh):
    rows, matrix, vector = P("fsdp", "ctx", None), P("fsdp", None), P("fsdp")
    cube = dict(mesh.shape) == {"ctx": 8, "fsdp": 4}
    return jax.shard_map(
        cube_body if cube else general_body,
        mesh=mesh,
        in_specs=(rows, vector, matrix, matrix, matrix, matrix, vector, matrix, matrix, matrix)
        + (rows, matrix, P()),
        out_specs=(rows, rows, vector, matrix, matrix, matrix, matrix, vector, matrix, matrix, matrix),
        check_vma=False,
    )
```

profile of v0, /device:TPU:17, one launch (start us, length us, event | category | flops | bytes accessed | tf_op | source)
XLA Modules:
  0.0 310.5 jit_solution(195515425597546923)
XLA Ops:
  0.7 0.7 stack.9
  1.3 0.7 stack.10
  2.0 0.1 tile.11
  2.1 0.6 tile.12.turns_ref
  2.7 0.6 fusion.6.gains_in
  3.3 139.7 %front.1 = (bf16[384,960]{1,0:T(8,128)(2,1)}, f32[384,128]{1,0:T(8,128)}, f32[384,128]{1,0:T(8,128)}, bf16[384,960]{1,0:T(8,128)(2,1)}, bf16[5,2,576,128]{3,2,1,...) custom-call(s32[16]{0:T(128)} %deal_ref.5, ...), custom_call_target="tpu_custom_call" | custom-call | tf_op jit(solution)/shard_map/front/pallas_call | solution.py:1155
  143.0 157.8 %back.1 = (bf16[384,960]{1,0:T(8,128)(2,1)}, f32[8,256]{1,0:T(8,128)}, bf16[20,240,128]{2,1,0:T(8,128)(2,1)}, bf16[2,20,240,128]{3,2,1,0:T(8,128)(2,1)}, bf16[8,640,128]{2,1,0:T(8,128)(2,1)}) custom-call(s32[16]{0:T(128)} %deal_ref.5, s32[1,2]{1,0:T(1,128)} %lengths_ref.3, bf16[5,2,576,128]{3,2,1,0:T(8,128)(2,1)} %get-tuple-element.43.q_ref, ...), custom_call_target="tpu_custom_call" | custom-call | tf_op jit(solution)/shard_map/back/pallas_call | solution.py:1216
  300.8 1.3 fusion.7
  302.2 7.9 %finish.1 = (bf16[960,384]{1,0:T(8,128)(2,1)}, bf16[960,384]{1,0:T(8,128)(2,1)}, f32[240,960]{1,0:T(8,128)}, f32[320,240]{1,0:T(8,128)}, f32[320,240]{1,0:T(8,12...) custom-call(s32[16]{0:T(128)} %deal_ref.5, ...), custom_call_target="tpu_custom_call" | custom-call | tf_op jit(solution)/shard_map/finish/pallas_call | solution.py:1257
  (2 shorter events, 0.0 us)
where the time goes:
time: 315 us; the launch traced here: 310 us
  Pallas kernels  305 us (97%)
  local copies, waits for them, and re-layouts  3.35 us (1%)
    pallas_call x1, Pallas kernels, cube_body(): pl.pallas_call(functools.partial(back_kernel, sizes, n, fsdp, ({}, {})),...  158 us
    pallas_call x1, Pallas kernels, cube_body(): pl.pallas_call(functools.partial(front_kernel, sizes, n, fsdp, ({}, {})),...  140 us
    pallas_call x1, Pallas kernels, cube_body(): pl.pallas_call(functools.partial(finish_kernel, heads), out_shape=(whole(...  7.88 us

commit v1 on v0

--- a/solution.py
+++ b/solution.py
@@ -121,6 +121,14 @@
     return jnp.concatenate([ref[t, rows, :] for t in tiles], axis=1)
 
 
+def flat_lanes(ref, tiles, shard):
+    stacked = [
+        jnp.concatenate([ref[zi, t * shard : (t + 1) * shard, :] for zi in range(ref.shape[0])], axis=0)
+        for t in tiles
+    ]
+    return jnp.concatenate(stacked, axis=1)
+
+
 def pack_tiles(parts):
     matrix = jnp.concatenate(parts, axis=1)
     short = -matrix.shape[1] % LANES
@@ -150,7 +158,18 @@
         return ref.at[:, pl.ds(0, self.rows)] if self.name == ATTN else ref
 
 
+class Flat:
+    def __init__(self, core):
+        self.core = core
+
+    def at(self, ref, zi, q):
+        size = ref.shape[1] // 8
+        return ref.at[zi, sub((2 * q + self.core) * size, size, 16)]
+
+
 PACKAGES = (ATTN, FF, DOWN)
+QKV, OUT = 3, 4
+GATHERED = (QKV, OUT, FF, DOWN)
 FINISH = 0
 
 
@@ -173,9 +192,13 @@
     z, chip = links.z, links.chip
     near, far = lax.bitwise_xor(chip, links.first), lax.bitwise_xor(chip, links.second)
     corner = lax.bitwise_xor(chip, 3)
-    shards = {ATTN: refs[ATTN].shape[1] // fsdp, FF: refs[FF].shape[2] // fsdp, DOWN: refs[DOWN].shape[1] // fsdp}
-    mine = {k: Share(k, core, shards[k]) for k in PACKAGES}
-    twin = {k: Share(k, 1 - core, shards[k]) for k in PACKAGES}
+    shards = {FF: refs[FF].shape[2] // fsdp, DOWN: refs[DOWN].shape[1] // fsdp}
+
+    def shares(core):
+        cut = {k: Share(k, core, shards[k]) for k in shards}
+        return {**cut, QKV: Flat(core), OUT: Flat(core)}
+
+    mine, twin = shares(core), shares(1 - core)
     stages = {}
 
     def over_z(k):
@@ -218,10 +241,10 @@
         for i in range(4):
             stages[FINISH, k, i]()
 
-    for k in PACKAGES:
+    for k in GATHERED:
         for i, q in ((0, chip), (1, far), (2, near), (3, corner)):
             stages[FINISH, k, i] = functools.partial(finish_some, k, i, q)
-    for k in PACKAGES:
+    for k in GATHERED:
         for fn in (over_z, spread, forward, pass_far, pass_corner, finish):
             stages[fn.__name__, k] = functools.partial(fn, k)
 
@@ -258,19 +281,22 @@
             links.send(("kv corner", b), SECOND, piece, piece)
             links.send(("kv core", 1, b), CORE, piece, piece)
 
-    def pass_on():
-        for i, (what, owner) in enumerate((("kv second", far), ("kv corner", corner))):
-            for b in range(2):
-                piece = kv_all.at[owner, b]
-                links.landed((what, b), piece)
-                links.send(("kv core", 2 + i, b), CORE, piece, piece)
-
-    def finish():
-        for i, owner in ((0, ctx), (1, far), (2, near), (3, corner)):
-            for b in range(2):
-                links.landed(("kv core", i, b), kv_all.at[lax.bitwise_xor(owner, 1), b])
-
-    return {"start": start, "forward": forward, "pass_on": pass_on, "finish": finish, "drain": links.drain}
+    def pass_some(i, what, owner):
+        for b in range(2):
+            piece = kv_all.at[owner, b]
+            links.landed((what, b), piece)
+            links.send(("kv core", i, b), CORE, piece, piece)
+
+    def finish(i, owner):
+        for b in range(2):
+            links.landed(("kv core", i, b), kv_all.at[lax.bitwise_xor(owner, 1), b])
+
+    stages = {"start": start, "forward": forward, "drain": links.drain}
+    stages["pass_far"] = functools.partial(pass_some, 2, "kv second", far)
+    stages["pass_corner"] = functools.partial(pass_some, 3, "kv corner", corner)
+    for i, owner in ((0, ctx), (1, far), (2, near), (3, corner)):
+        stages[FINISH, i] = functools.partial(finish, i, owner)
+    return stages
 
 
 def store_projection(sizes, raw_tiles, cos, sin, q_ref, kv_at):
@@ -346,7 +372,7 @@
     return own, other
 
 
-def attend_step(n, me, g, j, deal_ref, start_ref, q_ref, kv_ref, top_ref, acc_ref):
+def attend_step(n, me, g, at, deal_ref, start_ref, q_ref, kv_ref, top_ref, acc_ref):
     block = kv_ref.shape[3]
     rows = q_ref.shape[2]
     value_lane = lax.broadcasted_iota(jnp.int32, (block, LANES), 1) >= HD
@@ -364,44 +390,44 @@
         own0, own1 = kv_ref[me, 0, g], kv_ref[me, 1, g]
         s0 = scores(0, own0, own_mask(0))
         top0 = jnp.max(s0, axis=0, keepdims=True)
-        acc_ref[0] = weigh(s0, top0, own0)
-        top_ref[0] = jnp.broadcast_to(top0, top_ref.shape[1:])
+        acc_ref[g, 0] = weigh(s0, top0, own0)
+        top_ref[g, 0] = jnp.broadcast_to(top0, top_ref.shape[2:])
         s1 = scores(1, own1, own_mask(1))
         s2 = scores(1, own0, None)
         top1 = jnp.maximum(jnp.max(s1, axis=0, keepdims=True), jnp.max(s2, axis=0, keepdims=True))
-        acc_ref[1] = weigh(s1, top1, own1) + weigh(s2, top1, own0)
-        top_ref[1] = jnp.broadcast_to(top1, top_ref.shape[1:])
+        acc_ref[g, 1] = weigh(s1, top1, own1) + weigh(s2, top1, own0)
+        top_ref[g, 1] = jnp.broadcast_to(top1, top_ref.shape[2:])
 
     def other():
-        at = lax.rem(me + j, n)
         kind, mask = other_mask(at)
         is_prompt = kind == 0
-        tile0, tile1 = kv_ref[at, 0, g], kv_ref[at, kind, g]
+        tile0 = kv_ref[at, 0, g]
+        tile1 = jnp.where(is_prompt, tile0, kv_ref[at, 1, g])
         s1 = scores(1, tile0, None)
         s2 = scores(kind, tile1, mask)
-        old_p, old_c = top_ref[0, 0:1, :], top_ref[1, 0:1, :]
+        old_p, old_c = top_ref[g, 0, 0:1, :], top_ref[g, 1, 0:1, :]
         high1 = jnp.max(s1, axis=0, keepdims=True)
         high2 = jnp.max(s2, axis=0, keepdims=True)
         top_p = jnp.where(is_prompt, jnp.maximum(old_p, high2), old_p)
         top_c = jnp.maximum(old_c, jnp.where(is_prompt, high1, jnp.maximum(high1, high2)))
         part1 = weigh(s1, top_c, tile0)
         part2 = weigh(s2, jnp.where(is_prompt, top_p, top_c), tile1)
-        acc_ref[0] = acc_ref[0] * jnp.exp2((old_p - top_p) * LOG2E) + jnp.where(is_prompt, part2, 0.0)
-        acc_ref[1] = (
-            acc_ref[1] * jnp.exp2((old_c - top_c) * LOG2E) + part1 + jnp.where(is_prompt, 0.0, part2)
+        acc_ref[g, 0] = acc_ref[g, 0] * jnp.exp2((old_p - top_p) * LOG2E) + jnp.where(is_prompt, part2, 0.0)
+        acc_ref[g, 1] = (
+            acc_ref[g, 1] * jnp.exp2((old_c - top_c) * LOG2E) + part1 + jnp.where(is_prompt, 0.0, part2)
         )
-        top_ref[0] = jnp.broadcast_to(top_p, top_ref.shape[1:])
-        top_ref[1] = jnp.broadcast_to(top_c, top_ref.shape[1:])
+        top_ref[g, 0] = jnp.broadcast_to(top_p, top_ref.shape[2:])
+        top_ref[g, 1] = jnp.broadcast_to(top_c, top_ref.shape[2:])
 
     return own, other
 
 
 def attend_close(g, top_ref, acc_ref, o_ref, lse_ref):
     for b in range(2):
-        acc = acc_ref[b]
+        acc = acc_ref[g, b]
         total = acc[0:1, :]
         o_ref[g, b] = (acc / total).T
-        lse_ref[g, b] = jnp.broadcast_to(top_ref[b, 0:1, :] * LOG2E + jnp.log2(total), lse_ref.shape[2:])
+        lse_ref[g, b] = jnp.broadcast_to(top_ref[g, b, 0:1, :] * LOG2E + jnp.log2(total), lse_ref.shape[2:])
 
 
 def attend_back_step(n, me, g, j, deal_ref, start_ref, q_ref, kv_ref, do_ref, lse_ref, delta_ref, dqt_ref, dkv_ref):
@@ -461,10 +487,11 @@
     normed = (x * rms_inverse(x) * gain_row(gains_ref, 0, fsdp, x.shape[1] // fsdp)).astype(BF16)
     n1_ref[...] = normed
     count = -(-(heads + 2 * kvh) * HD // LANES)
+    shard = x.shape[1] // fsdp
     raw = []
     for t in range(0, count, 2):
         some = range(t, min(t + 2, count))
-        wide = nn(normed, lanes(attn_ref, some))
+        wide = nn(normed, flat_lanes(attn_ref, some, shard))
         raw += [wide[:, i * LANES : (i + 1) * LANES] for i in range(len(some))]
     store_projection(sizes, raw, cos_ref[...], sin_ref[...], q_ref, kv_at)
 
@@ -472,9 +499,9 @@
 def front_kernel(
     sizes, n, fsdp, plans, deal_ref, lengths_ref, xt_ref, gains_in, turns_ref,
     wq_ref, wkt_ref, wvt_ref, wo_ref, wg_ref, wu_ref, wdt_ref, cott_ref,
-    x_ref, cos_ref, sin_ref, n1_ref, q_ref, kv_out, lse_ref, gains_ref, attn_out,
+    x_ref, cos_ref, sin_ref, n1_ref, q_ref, kv_out, lse_ref, gains_ref, qkv_out,
     result_ref, gr_ref, do_ref, delta_ref, gain_ref, out_grad, ff_grad, down_grad,
-    attn, ff, down, kv_all, o_ref, gains, start_ref, top_ref, acc_ref, cot_ref,
+    qkv, wout, ff, down, kv_all, o_ref, gains, start_ref, top_ref, acc_ref, cot_ref,
     resid_ref, n2_ref, product_ref, gg_ref, gu_ref, turned_ref, gn_ref, out_stage, ff_stage, down_stage,
     send, recv, kv_send, kv_recv, local, out_sem,
 ):
@@ -482,18 +509,17 @@
     me, z = lax.axis_index("ctx"), lax.axis_index("fsdp")
     shard = wq_ref.shape[0]
     rows = sub(z * shard, shard, 16)
-    half = (heads + 2 * kvh) * HD % LANES
-    main = wo_ref.shape[1] - half
-    wo = wo_ref[...]
-    tiles = pack_tiles([wq_ref[...], wkt_ref[...].T, wvt_ref[...].T, wo[:, main:], wo[:, :main]])
-    for t, tile in enumerate(tiles):
-        attn[t, rows, :] = tile
+    for ref, parts in ((qkv, [wq_ref[...], wkt_ref[...].T, wvt_ref[...].T]), (wout, [wo_ref[...]])):
+        for t, tile in enumerate(pack_tiles(parts)):
+            ref[z, t * shard : (t + 1) * shard, :] = tile
+    used = -(-(heads + 2 * kvh) * HD // LANES) * shard
+    qkv[z, used:, :] = jnp.zeros((qkv.shape[1] - used, LANES), BF16)
     gains[z] = gains_in[...]
     greet("z", fsdp)
-    refs = {ATTN: attn, FF: ff, DOWN: down, "gains": gains}
+    refs = {QKV: qkv, OUT: wout, FF: ff, DOWN: down, "gains": gains}
     run = both_cores(lambda core: weight_stages(core, fsdp, plans[0], refs, send, recv))
     run_kv = both_cores(lambda core: kv_stages(core, plans[1], kv_all, kv_send, kv_recv))
-    run("gains_out", ("over_z", ATTN))
+    run("gains_out", ("over_z", QKV))
     for t in range(ff.shape[1]):
         ff[0, t, rows, :] = wg_ref[:, t * LANES : (t + 1) * LANES]
         ff[1, t, rows, :] = wu_ref[:, t * LANES : (t + 1) * LANES]
@@ -515,38 +541,52 @@
     sine = jnp.sin(angle)
     sin_ref[...] = jnp.where(lax.rem(lane, HD) < HD // 2, -sine, sine)
     start_ref[...] = first_keys(n, deal_ref, lengths_ref, block, start_ref.shape[1])
-    run(("spread", ATTN), ("over_z", DOWN), ("over_z", FF), ("forward", ATTN))
-    run(("pass_far", ATTN), ("pass_corner", ATTN))
-    run(("finish", ATTN), "gains_in")
+    run(("spread", QKV), ("over_z", OUT), ("over_z", DOWN), ("over_z", FF), ("forward", QKV))
+    run(("pass_far", QKV), ("pass_corner", QKV), ("finish", QKV), "gains_in")
     project(
-        sizes, fsdp, x_ref, gains, attn, cos_ref, sin_ref, n1_ref, q_ref,
+        sizes, fsdp, x_ref, gains, qkv, cos_ref, sin_ref, n1_ref, q_ref,
         lambda b, g: kv_all.at[me, b, g],
     )
-    run_kv("start", "forward")
-    run(("spread", DOWN))
-    run_kv("pass_on", "finish")
+    run_kv("start")
     gains_ref[...] = gains[...]
-    outs = [pltpu.make_async_copy(attn, attn_out, local.at[0]), pltpu.make_async_copy(kv_all, kv_out, local.at[1])]
-    for copy in outs:
-        copy.start()
+    outs = [pltpu.make_async_copy(qkv, qkv_out, local.at[0]), pltpu.make_async_copy(kv_all, kv_out, local.at[1])]
+    outs[0].start()
+    kv_schedule = {
+        kvh: ((FINISH, 0),),
+        2 * kvh: ("forward", "pass_far"),
+        4 * kvh: ((FINISH, 1), (FINISH, 2)),
+        6 * kvh: ("pass_corner",),
+        7 * kvh: ((FINISH, 3),),
+    }
     schedule = {
-        4: (("forward", DOWN),),
-        10: (("spread", FF),),
-        16: (("pass_far", DOWN), ("pass_corner", DOWN)),
-        24: (("forward", FF),),
-        30: (("finish", DOWN),),
-        38: (("pass_far", FF),),
+        3: (("spread", OUT),),
+        11: (("spread", DOWN),),
+        14: (("forward", OUT),),
+        18: (("forward", DOWN),),
+        20: (("spread", FF),),
+        24: (("pass_far", OUT), ("pass_corner", OUT)),
+        28: (("pass_far", DOWN), ("pass_corner", DOWN)),
+        32: (("forward", FF),),
+        38: (("finish", OUT), ("finish", DOWN)),
     }
 
     @pl.loop(0, kvh * n)
     def _(step):
-        g, j = step // n, step % n
+        j, g = step // kvh, step % kvh
+        turn = jnp.where(j == 3, 4, jnp.where(j == 4, 3, j))
+        for at, names in kv_schedule.items():
+            pl.when(step == at)(functools.partial(run_kv, *names))
         for at, names in schedule.items():
             pl.when(step == at)(functools.partial(run, *names))
-        own, other = attend_step(n, me, g, j, deal_ref, start_ref, q_ref, kv_all, top_ref, acc_ref)
+        own, other = attend_step(
+            n, me, g, lax.bitwise_xor(me, turn), deal_ref, start_ref, q_ref, kv_all, top_ref, acc_ref
+        )
         pl.when(j == 0)(own)
         pl.when(j > 0)(other)
         pl.when(j == n - 1)(lambda: attend_close(g, top_ref, acc_ref, o_ref, lse_ref))
+
+    outs[1].start()
+    run(("pass_far", FF))
 
     def quarter_ready(i):
         pl.when(i == 0)(lambda: run((FINISH, FF, 0)))
@@ -555,7 +595,7 @@
         return lax.bitwise_xor(me // 2, i)
 
     feed_forward(
-        sizes, fsdp, quarter_ready, lambda: None, x_ref, cot_ref, gains, attn, ff, down, o_ref,
+        sizes, fsdp, quarter_ready, x_ref, cot_ref, gains, wout, ff, down, o_ref,
         result_ref, gr_ref, do_ref, delta_ref, gain_ref, out_grad, ff_grad, down_grad,
         resid_ref, n2_ref, product_ref, gg_ref, gu_ref, turned_ref, gn_ref, out_stage, ff_stage, down_stage, out_sem,
     )
@@ -584,31 +624,38 @@
 
 
 def feed_forward(
-    sizes, fsdp, quarter_ready, all_ready, x_ref, cot_ref, gains_ref, attn_ref, ff_ref, down_ref, o_ref,
+    sizes, fsdp, quarter_ready, x_ref, cot_ref, gains_ref, wout_ref, ff_ref, down_ref, o_ref,
     result_ref, gr_ref, do_ref, delta_ref, gain_ref, out_grad, ff_grad, down_grad,
     resid_ref, n2_ref, product_ref, gg_ref, gu_ref, turned_ref, gn_ref, out_stage, ff_stage, down_stage, sem,
 ):
     heads, kvh, block = sizes
     share = heads // kvh
     rows, width = x_ref.shape
-    hidden = product_ref.shape[1]
-    mixed = (heads + 2 * kvh) * HD // LANES
+    shard = width // fsdp
     half = (heads + 2 * kvh) * HD % LANES
-    count = attn_ref.shape[0]
+    out_tiles = -(-width // LANES)
     down_tiles = down_ref.shape[0]
     gain = gain_row(gains_ref, 1, fsdp, width // fsdp)
     attended = head_columns(sizes, o_ref, HD).astype(BF16)
     pieces = []
-    for t in range(mixed, count, 2):
-        pieces.append(nn(attended, lanes(attn_ref, range(t, min(t + 2, count)))))
-    branch = jnp.concatenate(pieces, axis=1)
-    branch = jnp.concatenate([branch[:, LANES:], branch[:, half:LANES]], axis=1)
-    resid = x_ref[...].astype(F32) + branch
+    for t in range(0, out_tiles, 2):
+        pieces.append(nn(attended, flat_lanes(wout_ref, range(t, min(t + 2, out_tiles)), shard)))
+    resid = x_ref[...].astype(F32) + jnp.concatenate(pieces, axis=1)[:, :width]
     resid_ref[...] = resid
     n2_ref[...] = (resid * rms_inverse(resid) * gain).astype(BF16)
     pad = down_tiles * LANES - width
     wide = 2 * LANES
     per = ff_ref.shape[1] // 4
+    turned_ref[...] = n2_ref[...].T
+    gn_ref[...] = jnp.zeros(gn_ref.shape, F32)
+    gr_ref[...] = jnp.zeros(gr_ref.shape, F32)
+
+    def moves(q):
+        columns = sub(q * per * LANES, per * LANES, LANES)
+        return (
+            pltpu.make_async_copy(ff_stage, ff_grad.at[:, pl.ds(q * per, per)], sem.at[0]),
+            pltpu.make_async_copy(down_stage, down_grad.at[:, columns], sem.at[1]),
+        )
 
     @pl.loop(0, 4)
     def _(i):
@@ -617,54 +664,50 @@
         for low in range(0, per, 2):
             size = min(2, per - low)
             first = q * per + low
-            at = pl.ds(pl.multiple_of(first * LANES, LANES), size * LANES)
+            at = sub(first * LANES, size * LANES, LANES)
             n2 = n2_ref[...]
             gate = nn(n2, jnp.concatenate([ff_ref[0, first + t] for t in range(size)], axis=1))
             upward = nn(n2, jnp.concatenate([ff_ref[1, first + t] for t in range(size)], axis=1))
             grad = nt(cot_wide, jnp.concatenate([down_ref[t, at, :] for t in range(down_tiles)], axis=1))
             sigma = 1.0 / (1.0 + jnp.exp(-gate))
             activated = gate * sigma
-            product_ref[:, at] = (activated * upward).astype(BF16)
-            gg_ref[:, at] = (grad * upward * (sigma + activated * (1.0 - sigma))).astype(BF16)
-            gu_ref[:, at] = (grad * activated).astype(BF16)
-
-    all_ready()
-    for low in range(0, width, wide):
-        size = min(wide, width - low)
-        part = nt(gg_ref[...], lanes(ff_ref.at[0], range(hidden // LANES), slice(low, low + size)))
-        part = part + nt(gu_ref[...], lanes(ff_ref.at[1], range(hidden // LANES), slice(low, low + size)))
-        gn_ref[:, low : low + size] = part
-    turned_ref[...] = n2_ref[...].T
-
-    def ff_out(j):
-        return pltpu.make_async_copy(ff_stage.at[j % 2], ff_grad.at[:, pl.ds(2 * j, 2)], sem.at[j % 2])
-
-    def down_out(j):
-        at = pl.ds(pl.multiple_of(j * wide, wide), wide)
-        return pltpu.make_async_copy(down_stage.at[j % 2], down_grad.at[:, at], sem.at[2 + j % 2])
-
-    @pl.loop(0, hidden // wide)
-    def _(j):
-        at = pl.ds(pl.multiple_of(j * wide, wide), wide)
-        slot = lax.rem(j, 2)
-
-        @pl.when(j >= 2)
+            here = slice(low * LANES, (low + size) * LANES)
+            product_ref[:, here] = (activated * upward).astype(BF16)
+            gg_ref[:, here] = (grad * upward * (sigma + activated * (1.0 - sigma))).astype(BF16)
+            gu_ref[:, here] = (grad * activated).astype(BF16)
+        for low in range(0, width, wide):
+            size = min(wide, width - low)
+            part = 0.0
+            for c, grad_ref in enumerate((gg_ref, gu_ref)):
+                weights = [ff_ref[c, q * per + t, low : low + size, :] for t in range(per)]
+                part = part + nt(grad_ref[...], jnp.concatenate(weights, axis=1))
+            gn_ref[:, low : low + size] = gn_ref[:, low : low + size] + part
+        columns = sub(q * per * LANES, per * LANES, LANES)
+        for t in range(0, down_tiles, 2):
+            low, high = t * LANES, min((t + 2) * LANES, width)
+            weights = jnp.concatenate([down_ref[t, columns, :], down_ref[t + 1, columns, :]], axis=1)
+            part = nn(product_ref[...], weights)
+            gr_ref[:, low:high] = gr_ref[:, low:high] + part[:, : high - low]
+
+        @pl.when(i >= 1)
         def _():
-            ff_out(j - 2).wait()
-            down_out(j - 2).wait()
-
-        for c, grad_ref in enumerate((gg_ref, gu_ref)):
-            part = nn(turned_ref[...], grad_ref[:, at]).astype(BF16)
-            ff_stage[slot, c, 0] = part[:, :LANES]
-            ff_stage[slot, c, 1] = part[:, LANES:]
-        flipped = product_ref[:, at].T
-        cot_wide = jnp.concatenate([cot_ref[...], jnp.zeros((rows, pad), BF16)], axis=1)
-        part = nn(flipped, cot_wide).astype(BF16)
-        for t in range(down_tiles):
-            down_stage[slot, t] = part[:, t * LANES : (t + 1) * LANES]
-        ff_out(j).start()
-        down_out(j).start()
-
+            for copy in moves(q):
+                copy.wait()
+
+        for low in range(0, per, 2):
+            size = min(2, per - low)
+            here = slice(low * LANES, (low + size) * LANES)
+            for c, grad_ref in enumerate((gg_ref, gu_ref)):
+                part = nn(turned_ref[...], grad_ref[:, here]).astype(BF16)
+                for t in range(size):
+                    ff_stage[c, low + t] = part[:, t * LANES : (t + 1) * LANES]
+            part = nn(product_ref[:, here].T, cot_wide).astype(BF16)
+            for t in range(down_tiles):
+                down_stage[t, here, :] = part[:, t * LANES : (t + 1) * LANES]
+        for copy in moves(q):
+            copy.start()
+
+    result_ref[...] = (resid_ref[...] + gr_ref[...]).astype(BF16)
     grad_normed = gn_ref[...]
     resid = resid_ref[...]
     inverse = rms_inverse(resid)
@@ -679,18 +722,17 @@
     main = width - (LANES - half)
     lined = jnp.concatenate([jnp.zeros((rows, half), BF16), gb[:, main:], gb[:, :main]], axis=1)
     turned_ref[...] = head_columns(sizes, o_ref, HD).astype(BF16).T
-    for t in range(0, count - mixed, 2):
+    for t in range(0, out_tiles, 2):
         part = nn(turned_ref[...], lined[:, t * LANES : (t + 2) * LANES]).astype(BF16)
         out_stage[t] = part[:, :LANES]
         out_stage[t + 1] = part[:, LANES:]
-    out_copy = pltpu.make_async_copy(out_stage, out_grad, sem.at[4])
+    out_copy = pltpu.make_async_copy(out_stage, out_grad, sem.at[2])
     out_copy.start()
+    gb_wide = jnp.concatenate([gb, jnp.zeros((rows, out_tiles * LANES - width), BF16)], axis=1)
     grad_att = []
-    for low in range(0, width, wide):
-        size = min(wide, width - low)
-        grad_att.append(
-            nt(lined, lanes(attn_ref, range(mixed, count), slice(low, low + size))).astype(BF16)
-        )
+    for zi in range(fsdp):
+        weights = [wout_ref[zi, t * shard : (t + 1) * shard, :] for t in range(out_tiles)]
+        grad_att.append(nt(gb_wide, jnp.concatenate(weights, axis=1)).astype(BF16))
     grad_att = jnp.concatenate(grad_att, axis=1)
     zero = jnp.zeros((block, HD), BF16)
     for h in range(heads):
@@ -700,14 +742,8 @@
             )
     for g in range(kvh):
         row_deltas(g, do_ref, o_ref, delta_ref.at[g])
-    for t in range(0, down_tiles, 2):
-        low, high = t * LANES, min((t + 2) * LANES, width)
-        part = nn(product_ref[...], lanes(down_ref, (t, t + 1)))
-        result_ref[:, low:high] = (resid_ref[:, low:high] + part[:, : high - low]).astype(BF16)
-    last = hidden // wide
-    for j in (last - 2, last - 1):
-        ff_out(j).wait()
-        down_out(j).wait()
+    for copy in moves(0):
+        copy.wait()
     out_copy.wait()
 
 
@@ -738,6 +774,9 @@
     twin = {k: Share(k, 1 - core, shards[k]) for k in PACKAGES}
     stages = {}
 
+    def slot_of(d):
+        return max(d - 1, 0)
+
     def hold(k, d, q):
         if k in held:
             return held[k].at[d, q]
@@ -762,23 +801,34 @@
             links.landed((k, CORE, d, q), share.buffer(got[k][0].at[d, q]))
             if k in held:
                 load(k, d, q).wait()
-            add_rows(hold(k, d, q), (hold(k, d, q), got[k][0].at[d, q]), share.rows)
+            terms = [hold(k, d, q), got[k][0].at[d, q]]
+            if d == 0:
+                links.landed((k, "direct", q), share.buffer(got[k][4].at[q]))
+                terms.append(got[k][4].at[q])
+            add_rows(hold(k, d, q), terms, share.rows)
+            if d == 1:
+                links.send((k, "direct", q), d, hold(k, d, q), share.buffer(got[k][4].at[q]))
         for i, q in enumerate((near, corner)):
-            links.send((k, FIRST, d, i), FIRST, hold(k, d, q), share.buffer(got[k][1].at[d, i]))
+            if d != 1:
+                links.send((k, FIRST, d, i), FIRST, hold(k, d, q), share.buffer(got[k][1].at[slot_of(d), i]))
 
     def stage2(k, d):
-        share = mine[k]
+        share, slot = mine[k], slot_of(d)
+        if d == 1:
+            return
         for i in range(2):
-            links.landed((k, FIRST, d, i), share.buffer(got[k][1].at[d, i]))
-        add_rows(hold(k, d, far), (hold(k, d, far), got[k][1].at[d, 1]), share.rows)
-        links.send((k, SECOND, d), SECOND, hold(k, d, far), share.buffer(got[k][2].at[d]))
+            links.landed((k, FIRST, d, i), share.buffer(got[k][1].at[slot, i]))
+        add_rows(hold(k, d, far), (hold(k, d, far), got[k][1].at[slot, 1]), share.rows)
+        links.send((k, SECOND, d), SECOND, hold(k, d, far), share.buffer(got[k][2].at[slot]))
 
     def stage3(k, d):
-        share = mine[k]
-        links.landed((k, SECOND, d), share.buffer(got[k][2].at[d]))
-        add_rows(hold(k, d, chip), (hold(k, d, chip), got[k][1].at[d, 0], got[k][2].at[d]), share.rows)
+        share, slot = mine[k], slot_of(d)
+        if d == 1:
+            return
+        links.landed((k, SECOND, d), share.buffer(got[k][2].at[slot]))
+        add_rows(hold(k, d, chip), (hold(k, d, chip), got[k][1].at[slot, 0], got[k][2].at[slot]), share.rows)
         if d > 0:
-            links.send((k, "z", d), d, hold(k, d, chip), share.buffer(got[k][3].at[d - 1]))
+            links.send((k, "z", d), d, hold(k, d, chip), share.buffer(got[k][3].at[d - 2]))
 
     def out_copy(k):
         slot = len(PACKAGES) * fsdp * 4 + PACKAGES.index(k)
@@ -786,10 +836,10 @@
 
     def close(k):
         share = mine[k]
-        for d in range(1, fsdp):
-            links.landed((k, "z", d), share.buffer(got[k][3].at[d - 1]))
+        for d in range(2, fsdp):
+            links.landed((k, "z", d), share.buffer(got[k][3].at[d - 2]))
         final = hold(k, 0, chip)
-        add_rows(final, [final] + [got[k][3].at[d - 1] for d in range(1, fsdp)], share.rows)
+        add_rows(final, [final] + [got[k][3].at[d - 2] for d in range(2, fsdp)], share.rows)
         for hop in (FIRST, SECOND):
             links.send((k, "out", hop), hop, final, share.at(outs[k], 0, chip))
         links.send((k, "out core", 0), CORE, final, share.at(outs[k], 0, chip))
@@ -886,10 +936,10 @@
 
 def back_kernel(
     sizes, n, fsdp, plans, deal_ref, lengths_ref, q_ref, kv_in, do_ref, delta_ref, lse_ref,
-    x_ref, n1_ref, gr_ref, gains_ref, gain_two_ref, cos_ref, sin_ref, attn_ref, out_grad_ref, ff_grad, down_grad,
+    x_ref, n1_ref, gr_ref, gains_ref, gain_two_ref, cos_ref, sin_ref, qkv_ref, out_grad_ref, ff_grad, down_grad,
     tg_ref, gain_out, attn_out, ff_out, down_out,
     start_ref, spill_ref, chunk_ref, dqt_ref, dq_ref, dkv_ref, kv_sum, kv_got0, kv_got1, kv_got2, gp_ref, gn_ref, turned_ref, attn_grad,
-    ff_a, down_a, attn_0, ff_0, down_0, attn_1, ff_1, down_1, attn_2, ff_2, down_2, attn_3, ff_3, down_3,
+    ff_a, down_a, attn_0, ff_0, down_0, attn_1, ff_1, down_1, attn_2, ff_2, down_2, attn_3, ff_3, down_3, attn_4, ff_4, down_4,
     gain_sum, gain_got, gain_z, send, recv, kv_send, kv_recv, local, ahead_sem,
 ):
     heads, kvh, block = sizes
@@ -900,7 +950,11 @@
     greet("z", fsdp)
     sources = {ATTN: attn_grad, FF: ff_grad, DOWN: down_grad}
     held = {FF: ff_a, DOWN: down_a}
-    got = {ATTN: (attn_0, attn_1, attn_2, attn_3), FF: (ff_0, ff_1, ff_2, ff_3), DOWN: (down_0, down_1, down_2, down_3)}
+    got = {
+        ATTN: (attn_0, attn_1, attn_2, attn_3, attn_4),
+        FF: (ff_0, ff_1, ff_2, ff_3, ff_4),
+        DOWN: (down_0, down_1, down_2, down_3, down_4),
+    }
     outs = {ATTN: attn_out, FF: ff_out, DOWN: down_out}
     run = both_cores(
         lambda core: grad_stages(
@@ -938,14 +992,9 @@
             attn_grad.at[pl.ds(width_tiles, attn_grad.shape[0] - width_tiles)], ahead_sem.at[1],
         ),
     ]
-    wide = 2 * LANES
-
     def weight_rows(i):
-        size = min(wide, width - i * wide)
-        return pltpu.make_async_copy(
-            attn_ref.at[pl.ds(0, width_tiles), pl.ds(i * wide, size)],
-            chunk_ref.at[i % 2, :, pl.ds(0, size)], ahead_sem.at[2 + i % 2],
-        )
+        size = chunk_ref.shape[1]
+        return pltpu.make_async_copy(qkv_ref.at[i, pl.ds(0, size)], chunk_ref.at[i % 2], ahead_sem.at[2 + i % 2])
 
     for copy in ahead + [weight_rows(0), weight_rows(1)]:
         copy.start()
@@ -1016,13 +1065,15 @@
     run_kv(*[key for key in late[1:] if key[0] >= 2 and key[1] == kvh - 1])
     some_tiles(heads // 2, tiles)
     run(("begin", ATTN, order[0]), ("begin", ATTN, order[1]), ("stage1", ATTN, order[0]), *rest[1])
-    for i in range(-(-width // wide)):
-        size = min(wide, width - i * wide)
+    shard = width // fsdp
+    pieces = []
+    for i in range(fsdp):
         weight_rows(i).wait()
-        rows_in = jnp.concatenate([chunk_ref[i % 2, t, 0:size, :] for t in range(tiles)], axis=1)
-        gn_ref[:, i * wide : i * wide + size] = nt(gp_ref[...], rows_in)
-        if (i + 2) * wide < width:
+        rows_in = jnp.concatenate([chunk_ref[i % 2, t * shard : (t + 1) * shard, :] for t in range(tiles)], axis=1)
+        pieces.append(nt(gp_ref[...], rows_in))
+        if i + 2 < fsdp:
             weight_rows(i + 2).start()
+    gn_ref[...] = jnp.concatenate(pieces, axis=1)
     x = x_ref[...].astype(F32)
     inverse = rms_inverse(x)
     scaled = x * inverse
@@ -1030,7 +1081,6 @@
     weighted = grad_normed * gain_row(gains_ref, 0, fsdp, width // fsdp)
     gain_one = jnp.sum(grad_normed * scaled, axis=0, keepdims=True)
     gain_two = gain_two_ref[0:1, :]
-    shard = width // fsdp
     tail = gain_sum.shape[3] - shard
     for i in range(fsdp):
         both = jnp.concatenate(
@@ -1148,9 +1198,10 @@
     kv_shape = (n, 2, kvh, block, LANES)
     dma = pltpu.SemaphoreType.DMA
     mixed = (width + 2 * kv_width) // LANES
-    wide = 2 * LANES
+    qkv_tiles = -(-(width + 2 * kv_width) // LANES)
+    qkv_shape = (fsdp, -(-qkv_tiles * shard // LANES) * LANES, LANES)
     (
-        x, cos, sin, normed_one, q, kv_all, lse, gains, w_attn,
+        x, cos, sin, normed_one, q, kv_all, lse, gains, w_qkv,
         result, grad_resid, grad_heads, deltas, gain_two, out_grad, ff_grad, down_grad,
     ) = pl.pallas_call(
         functools.partial(front_kernel, sizes, n, fsdp, ({}, {})),
@@ -1163,7 +1214,7 @@
             whole(kv_shape, BF16),
             whole(row_shape, F32),
             whole(gain_shape, F32),
-            whole((attn_tiles, fsdp * shard, LANES), BF16),
+            whole(qkv_shape, BF16),
             whole((row_count, width), BF16),
             whole((row_count, width), F32),
             whole(heads_shape, BF16),
@@ -1176,27 +1227,28 @@
         in_specs=[SMEM] * 2 + [VMEM] * 11,
         out_specs=(VMEM,) * 5 + (ANY, VMEM, VMEM, ANY) + (VMEM,) * 5 + (ANY,) * 3,
         scratch_shapes=[
-            pltpu.VMEM((attn_tiles, fsdp * shard, LANES), BF16),
+            pltpu.VMEM(qkv_shape, BF16),
+            pltpu.VMEM((fsdp, down_tiles * shard, LANES), BF16),
             pltpu.VMEM((2, ff_tiles, fsdp * shard, LANES), BF16),
             pltpu.VMEM((down_tiles, fsdp * down_shard, LANES), BF16),
             pltpu.VMEM(kv_shape, BF16),
             pltpu.VMEM(heads_shape, F32),
             pltpu.VMEM(gain_shape, F32),
             pltpu.VMEM((8, stack), jnp.int32),
-            pltpu.VMEM((2, 8, stack), F32),
-            pltpu.VMEM((2, LANES, stack), F32),
+            pltpu.VMEM((kvh, 2, 8, stack), F32),
+            pltpu.VMEM((kvh, 2, LANES, stack), F32),
             pltpu.VMEM((row_count, width), BF16),
             pltpu.VMEM((row_count, width), F32),
             pltpu.VMEM((row_count, width), BF16),
-            pltpu.VMEM((row_count, hidden), BF16),
-            pltpu.VMEM((row_count, hidden), BF16),
-            pltpu.VMEM((row_count, hidden), BF16),
+            pltpu.VMEM((row_count, hidden // 4), BF16),
+            pltpu.VMEM((row_count, hidden // 4), BF16),
+            pltpu.VMEM((row_count, hidden // 4), BF16),
             pltpu.VMEM((width, row_count), BF16),
             pltpu.VMEM((row_count, width), F32),
             pltpu.VMEM((attn_tiles - mixed, width, LANES), BF16),
-            pltpu.VMEM((2, 2, 2, width, LANES), BF16),
-            pltpu.VMEM((2, down_tiles, wide, LANES), BF16),
-            dma((75,)), dma((75,)), dma((14,)), dma((14,)), dma((2,)), dma((5,)),
+            pltpu.VMEM((2, ff_tiles // 4, width, LANES), BF16),
+            pltpu.VMEM((down_tiles, hidden // 4, LANES), BF16),
+            dma((99,)), dma((99,)), dma((14,)), dma((14,)), dma((2,)), dma((3,)),
         ],
         compiler_params=params(0),
         name="front",
@@ -1209,9 +1261,8 @@
     attn_rows = -(-shard // 32) * 16
     shapes = ((attn_tiles // 4, attn_rows, LANES), (ff_tiles // 4, shard, LANES), (down_shard, LANES))
     buffers = [pltpu.VMEM((fsdp, 4) + shape, BF16) for shape in shapes[1:]]
-    for lead in ((fsdp, 4), (fsdp, 2), (fsdp,), (fsdp - 1,)):
+    for lead in ((fsdp, 4), (fsdp - 1, 2), (fsdp - 1,), (fsdp - 2,), (4,)):
         buffers += [pltpu.VMEM(lead + shape, BF16) for shape in shapes]
-    qkv_tiles = -(-(width + 2 * kv_width) // LANES)
     piece = (2, block, LANES)
     tokens_grad, gain_grads, attn_w, ff_w, down_w = pl.pallas_call(
         functools.partial(back_kernel, sizes, n, fsdp, ({}, {})),
@@ -1227,7 +1278,7 @@
         scratch_shapes=[
             pltpu.VMEM((8, stack), jnp.int32),
             pltpu.VMEM((width, LANES), BF16),
-            pltpu.VMEM((2, qkv_tiles, 2 * LANES, LANES), BF16),
+            pltpu.VMEM((2, qkv_tiles * shard, LANES), BF16),
             pltpu.VMEM((2, LANES, stack), F32),
             pltpu.VMEM((kvh, stack, LANES), F32),
             pltpu.VMEM((n, kvh) + piece, BF16),
@@ -1245,13 +1296,13 @@
             pltpu.VMEM((4,) + gain_shape, F32),
             pltpu.VMEM((3,) + gain_shape, F32),
             pltpu.VMEM((fsdp - 1,) + gains_in.shape, F32),
-            dma((120,)), dma((120,)), dma((7 * kvh,)), dma((7 * kvh,)), dma((51,)), dma((4,)),
+            dma((123,)), dma((123,)), dma((7 * kvh,)), dma((7 * kvh,)), dma((51,)), dma((4,)),
         ],
         compiler_params=params(1),
         name="back",
     )(
         block_deal, cont_lengths, q, kv_all, grad_heads, deltas, lse, x, normed_one, grad_resid, gains, gain_two,
-        cos, sin, w_attn, out_grad, ff_grad, down_grad,
+        cos, sin, w_qkv, out_grad, ff_grad, down_grad,
     )
 
     out_t, tg_t, q_w, k_t, v_t, o_w, gate_w, up_w, d_t = pl.pallas_call(

time: 315 us -> 293 us (0.930)
  Pallas kernels: 305 us -> 283 us
    pallas_call x1, Pallas kernels: 158 us -> 146 us  [cube_body(): pl.pallas_call(functools.partial(back_kernel, sizes, n, fsdp, ({}, {})),...]
    pallas_call x1, Pallas kernels: 140 us -> 129 us  [cube_body(): pl.pallas_call(functools.partial(front_kernel, sizes, n, fsdp, ({}, {})),...]
where the time goes in v1:
time: 293 us; the launch traced here: 289 us
  Pallas kernels  283 us (97%)
  local copies, waits for them, and re-layouts  3.35 us (1%)
    pallas_call x1, Pallas kernels, cube_body(): pl.pallas_call(functools.partial(back_kernel, sizes, n, fsdp, ({}, {})),...  146 us
    pallas_call x1, Pallas kernels, cube_body(): pl.pallas_call(functools.partial(front_kernel, sizes, n, fsdp, ({}, {})),...  129 us
    pallas_call x1, Pallas kernels, cube_body(): pl.pallas_call(functools.partial(finish_kernel, heads), out_shape=(whole(...  7.88 us

profile of v1, /device:TPU:17, one launch (start us, length us, event | category | flops | bytes accessed | tf_op | source)
XLA Modules:
  0.0 288.5 jit_solution(9980132467110459335)
XLA Ops:
  0.7 0.7 stack.9
  1.3 0.7 stack.10
  2.0 0.1 tile.11
  2.1 0.6 tile.12.turns_ref
  2.7 0.6 fusion.6.gains_in
  3.3 129.1 %front.1 = (bf16[384,960]{1,0:T(8,128)(2,1)}, f32[384,128]{1,0:T(8,128)}, f32[384,128]{1,0:T(8,128)}, bf16[384,960]{1,0:T(8,128)(2,1)}, bf16[5,2,576,128]{3,2,1,...) custom-call(s32[16]{0:T(128)} %deal_ref.5, ...), custom_call_target="tpu_custom_call" | custom-call | tf_op jit(solution)/shard_map/front/pallas_call | solution.py:1206
  132.3 146.5 %back.1 = (bf16[384,960]{1,0:T(8,128)(2,1)}, f32[8,256]{1,0:T(8,128)}, bf16[20,240,128]{2,1,0:T(8,128)(2,1)}, bf16[2,20,240,128]{3,2,1,0:T(8,128)(2,1)}, bf16[8,640,128]{2,1,0:T(8,128)(2,1)}) custom-call(s32[16]{0:T(128)} %deal_ref.5, s32[1,2]{1,0:T(1,128)} %lengths_ref.3, bf16[5,2,576,128]{3,2,1,0:T(8,128)(2,1)} %get-tuple-element.43.q_ref, ...), custom_call_target="tpu_custom_call" | custom-call | tf_op jit(solution)/shard_map/back/pallas_call | solution.py:1267
  278.8 1.3 fusion.7
  280.2 7.9 %finish.1 = (bf16[960,384]{1,0:T(8,128)(2,1)}, bf16[960,384]{1,0:T(8,128)(2,1)}, f32[240,960]{1,0:T(8,128)}, f32[320,240]{1,0:T(8,128)}, f32[320,240]{1,0:T(8,12...) custom-call(s32[16]{0:T(128)} %deal_ref.5, ...), custom_call_target="tpu_custom_call" | custom-call | tf_op jit(solution)/shard_map/finish/pallas_call | solution.py:1308
  (2 shorter events, 0.0 us)

commit v2 on v1

--- a/solution.py
+++ b/solution.py
@@ -999,8 +999,8 @@
     for copy in ahead + [weight_rows(0), weight_rows(1)]:
         copy.start()
     total = kvh * n
-    pace = 12
-    kv_due = sorted((8 * (i + 1) + (0, 3, 11, 19)[stage], stage, i) for i in range(kvh) for stage in range(4))
+    pace = 9
+    kv_due = sorted((8 * (i + 1) + (0, 3, 15, 27)[stage], stage, i) for i in range(kvh) for stage in range(4))
 
     @pl.loop(0, total)
     def _(step):

time: 293 us -> 288 us (0.983)
  Pallas kernels: 283 us -> 278 us
    pallas_call x1, Pallas kernels: 146 us -> 141 us  [cube_body(): pl.pallas_call(functools.partial(back_kernel, sizes, n, fsdp, ({}, {})),...]
where the time goes in v2:
time: 288 us; the launch traced here: 283 us
  Pallas kernels  278 us (97%)
  local copies, waits for them, and re-layouts  3.35 us (1%)
    pallas_call x1, Pallas kernels, cube_body(): pl.pallas_call(functools.partial(back_kernel, sizes, n, fsdp, ({}, {})),...  141 us
    pallas_call x1, Pallas kernels, cube_body(): pl.pallas_call(functools.partial(front_kernel, sizes, n, fsdp, ({}, {})),...  129 us
    pallas_call x1, Pallas kernels, cube_body(): pl.pallas_call(functools.partial(finish_kernel, heads), out_shape=(whole(...  7.88 us

profile of v2, /device:TPU:17, one launch (start us, length us, event | category | flops | bytes accessed | tf_op | source)
XLA Modules:
  0.0 282.9 jit_solution(9257290084365946673)
XLA Ops:
  0.7 0.7 stack.9
  1.3 0.7 stack.10
  2.0 0.1 tile.11
  2.1 0.6 tile.12.turns_ref
  2.7 0.6 fusion.6.gains_in
  3.3 129.1 %front.1 = (bf16[384,960]{1,0:T(8,128)(2,1)}, f32[384,128]{1,0:T(8,128)}, f32[384,128]{1,0:T(8,128)}, bf16[384,960]{1,0:T(8,128)(2,1)}, bf16[5,2,576,128]{3,2,1,...) custom-call(s32[16]{0:T(128)} %deal_ref.5, ...), custom_call_target="tpu_custom_call" | custom-call | tf_op jit(solution)/shard_map/front/pallas_call | solution.py:1206
  132.3 140.9 %back.1 = (bf16[384,960]{1,0:T(8,128)(2,1)}, f32[8,256]{1,0:T(8,128)}, bf16[20,240,128]{2,1,0:T(8,128)(2,1)}, bf16[2,20,240,128]{3,2,1,0:T(8,128)(2,1)}, bf16[8,640,128]{2,1,0:T(8,128)(2,1)}) custom-call(s32[16]{0:T(128)} %deal_ref.5, s32[1,2]{1,0:T(1,128)} %lengths_ref.3, bf16[5,2,576,128]{3,2,1,0:T(8,128)(2,1)} %get-tuple-element.43.q_ref, ...), custom_call_target="tpu_custom_call" | custom-call | tf_op jit(solution)/shard_map/back/pallas_call | solution.py:1267
  273.2 1.3 fusion.7
  274.5 7.9 %finish.1 = (bf16[960,384]{1,0:T(8,128)(2,1)}, bf16[960,384]{1,0:T(8,128)(2,1)}, f32[240,960]{1,0:T(8,128)}, f32[320,240]{1,0:T(8,128)}, f32[320,240]{1,0:T(8,12...) custom-call(s32[16]{0:T(128)} %deal_ref.5, ...), custom_call_target="tpu_custom_call" | custom-call | tf_op jit(solution)/shard_map/finish/pallas_call | solution.py:1308
  (2 shorter events, 0.0 us)

commit v3 on v2

--- a/solution.py
+++ b/solution.py
@@ -2,6 +2,7 @@
 
 import jax
 import jax.numpy as jnp
+import numpy as np
 from jax import lax
 from jax.experimental import pallas as pl
 from jax.experimental.pallas import tpu as pltpu
@@ -497,7 +498,7 @@
 
 
 def front_kernel(
-    sizes, n, fsdp, plans, deal_ref, lengths_ref, xt_ref, gains_in, turns_ref,
+    sizes, n, fsdp, plans, deal_ref, lengths_ref, xt_ref, gain_one_in, gain_two_in, turns_ref,
     wq_ref, wkt_ref, wvt_ref, wo_ref, wg_ref, wu_ref, wdt_ref, cott_ref,
     x_ref, cos_ref, sin_ref, n1_ref, q_ref, kv_out, lse_ref, gains_ref, qkv_out,
     result_ref, gr_ref, do_ref, delta_ref, gain_ref, out_grad, ff_grad, down_grad,
@@ -514,7 +515,9 @@
             ref[z, t * shard : (t + 1) * shard, :] = tile
     used = -(-(heads + 2 * kvh) * HD // LANES) * shard
     qkv[z, used:, :] = jnp.zeros((qkv.shape[1] - used, LANES), BF16)
-    gains[z] = gains_in[...]
+    gains[z] = jnp.zeros(gains.shape[1:], F32)
+    for i, ref in enumerate((gain_one_in, gain_two_in)):
+        gains[z, i : i + 1, 0:shard] = ref[...].astype(F32)
     greet("z", fsdp)
     refs = {QKV: qkv, OUT: wout, FF: ff, DOWN: down, "gains": gains}
     run = both_cores(lambda core: weight_stages(core, fsdp, plans[0], refs, send, recv))
@@ -970,14 +973,14 @@
     steps = []
     for i in range(len(chunks) + 7):
         names = []
-        if i + 1 < len(chunks):
-            names.append(("begin",) + chunks[i + 1])
         if i < len(chunks):
             names.append(("stage1",) + chunks[i])
         if 1 <= i <= len(chunks):
             names.append(("stage2",) + chunks[i - 1])
         if 2 <= i <= len(chunks) + 1:
             names.append(("stage3",) + chunks[i - 2])
+        if i + 1 < len(chunks):
+            names.insert(1, ("begin",) + chunks[i + 1])
         for last, k in ((len(order) + 1, FF), (len(chunks) + 1, DOWN)):
             for extra, what in enumerate(("close", "close2", "close3", "close4")):
                 if i == last + 1 + extra:
@@ -1185,11 +1188,10 @@
     share = heads // kvh
     stack = share * block
     sizes = (heads, kvh, block)
-    half_turns = THETA ** (-2.0 * jnp.arange(HD // 2, dtype=F32) / HD)
-    turns = jnp.tile(half_turns, (8, LANES // (HD // 2)))
+    turns = np.tile(THETA ** (-2.0 * np.arange(HD // 2) / HD), (8, LANES // (HD // 2))).astype(np.float32)
     pad = -shard % LANES
-    gains_in = jnp.pad(jnp.stack([attn_gain, mlp_gain]).astype(F32), ((0, 6), (0, pad)))
-    gain_shape = (fsdp,) + gains_in.shape
+    gains_shape = (8, shard + pad)
+    gain_shape = (fsdp,) + gains_shape
     attn_tiles = (2 * width + 2 * kv_width) // LANES
     ff_tiles = hidden // LANES
     down_tiles = -(-width // LANES)
@@ -1224,7 +1226,7 @@
             whole((2, ff_tiles, width, LANES), BF16),
             whole((down_tiles, hidden, LANES), BF16),
         ),
-        in_specs=[SMEM] * 2 + [VMEM] * 11,
+        in_specs=[SMEM] * 2 + [VMEM] * 12,
         out_specs=(VMEM,) * 5 + (ANY, VMEM, VMEM, ANY) + (VMEM,) * 5 + (ANY,) * 3,
         scratch_shapes=[
             pltpu.VMEM(qkv_shape, BF16),
@@ -1253,7 +1255,7 @@
         compiler_params=params(0),
         name="front",
     )(
-        block_deal, cont_lengths, tokens[0].T, gains_in, turns,
+        block_deal, cont_lengths, tokens[0].T, attn_gain[None], mlp_gain[None], turns,
         query_weight, key_weight.T, value_weight.T, out_weight, gate_weight, up_weight, down_weight.T,
         cotangent[0].T,
     )
@@ -1268,7 +1270,7 @@
         functools.partial(back_kernel, sizes, n, fsdp, ({}, {})),
         out_shape=(
             whole((row_count, width), BF16),
-            whole(gains_in.shape, F32),
+            whole(gains_shape, F32),
             whole((attn_tiles, shard, LANES), BF16),
             whole((2, ff_tiles, shard, LANES), BF16),
             whole((down_tiles, down_shard, LANES), BF16),
@@ -1295,7 +1297,7 @@
         + [
             pltpu.VMEM((4,) + gain_shape, F32),
             pltpu.VMEM((3,) + gain_shape, F32),
-            pltpu.VMEM((fsdp - 1,) + gains_in.shape, F32),
+            pltpu.VMEM((fsdp - 1,) + gains_shape, F32),
             dma((123,)), dma((123,)), dma((7 * kvh,)), dma((7 * kvh,)), dma((51,)), dma((4,)),
         ],
         compiler_params=params(1),

time: 288 us -> 288 us (level)
  no operation moved by 1% of the time
where the time goes in v3:
time: 288 us; the launch traced here: 283 us
  Pallas kernels  278 us (97%)
  local copies, waits for them, and re-layouts  3.78 us (1%)
    pallas_call x1, Pallas kernels, cube_body(): pl.pallas_call(functools.partial(back_kernel, sizes, n, fsdp, ({}, {})),...  141 us
    pallas_call x1, Pallas kernels, cube_body(): pl.pallas_call(functools.partial(front_kernel, sizes, n, fsdp, ({}, {})),...  129 us
    pallas_call x1, Pallas kernels, cube_body(): pl.pallas_call(functools.partial(finish_kernel, heads), out_shape=(whole(...  7.88 us

profile of v3, /device:TPU:17, one launch (start us, length us, event | category | flops | bytes accessed | tf_op | source)
XLA Modules:
  0.0 283.3 jit_solution(10534862027056258112)
XLA Ops:
  0.6 1.2 broadcast_in_dim.12.gain_one_in
  1.9 1.2 broadcast_in_dim.13.gain_two_in
  3.1 129.1 %front.1 = (bf16[384,960]{1,0:T(8,128)(2,1)}, f32[384,128]{1,0:T(8,128)}, f32[384,128]{1,0:T(8,128)}, bf16[384,960]{1,0:T(8,128)(2,1)}, bf16[5,2,576,128]{3,2,1,...) custom-call(s32[16]{0:T(128)} %deal_ref.5, ...), custom_call_target="tpu_custom_call" | custom-call | tf_op jit(solution)/shard_map/front/pallas_call | solution.py:1208
  132.2 141.4 %back.1 = (bf16[384,960]{1,0:T(8,128)(2,1)}, f32[8,256]{1,0:T(8,128)}, bf16[20,240,128]{2,1,0:T(8,128)(2,1)}, bf16[2,20,240,128]{3,2,1,0:T(8,128)(2,1)}, bf16[8,640,128]{2,1,0:T(8,128)(2,1)}) custom-call(s32[16]{0:T(128)} %deal_ref.5, s32[1,2]{1,0:T(1,128)} %lengths_ref.3, bf16[5,2,576,128]{3,2,1,0:T(8,128)(2,1)} %get-tuple-element.43.q_ref, ...), custom_call_target="tpu_custom_call" | custom-call | tf_op jit(solution)/shard_map/back/pallas_call | solution.py:1269
  273.6 1.3 fusion
  275.0 7.9 %finish.1 = (bf16[960,384]{1,0:T(8,128)(2,1)}, bf16[960,384]{1,0:T(8,128)(2,1)}, f32[240,960]{1,0:T(8,128)}, f32[320,240]{1,0:T(8,128)}, f32[320,240]{1,0:T(8,12...) custom-call(s32[16]{0:T(128)} %deal_ref.5, ...), custom_call_target="tpu_custom_call" | custom-call | tf_op jit(solution)/shard_map/finish/pallas_call | solution.py:1310
